TPU v7x, 512 devices: a whole 4x4x16 slice. The times are simulated.
512 devices in a mesh: tm: 64 (over z, x_hi, core), groups: 8 (over y, x_lo).
Axes of the slice: x: 4 (x_hi: 2, x_lo: 2; x = x_hi * 2 + x_lo), y: 4, z: 16, core: 2. Of those that a mesh axis runs over, the one named last changes fastest.
Arguments:
- queries: bfloat16 [65536, 256], P(('groups', 'tm')), parts along dimension 0, may hold values from -6 to 6
- keys: bfloat16 [65536, 256], P(('groups', 'tm')), parts along dimension 0, may hold values from -6 to 6
- values: bfloat16 [65536, 256], P(('groups', 'tm')), parts along dimension 0, may hold values from -6 to 6
- out_grad: bfloat16 [65536, 256], P(('groups', 'tm')), parts along dimension 0, may hold values from -6 to 6
- key_blocks: int32 [512, 6], P(('groups', 'tm')), parts along dimension 0, may hold values from -1 to 63, as said below
Outputs:
- query_grad: bfloat16 [65536, 256], P(('groups', 'tm')), parts along dimension 0
- key_grad: bfloat16 [65536, 256], P(('groups', 'tm')), parts along dimension 0
- value_grad: bfloat16 [65536, 256], P(('groups', 'tm')), parts along dimension 0
There are 8 independent parts, one for each index of `groups`. A program takes and returns all parts, laid end to end along the dimension named above; each array names one. Nothing has to cross between parts.
Inputs may be any that keep to these rules, and one draw needn't show every extreme that they name: `key_blocks`: slot d of row i holds either (i - d) mod 64 or -1; slots 0 to 3 are never -1; some row has no -1, and some row has -1 in every slot from 4 on.
All inputs are finite; a program needn't handle non-finite values.
Results may differ from a plain program's by a relative error of at most 0.033.
Values may be sent and summed in bfloat16 or wider, within the bound.
No kernel may reach another device: no remote copies, remote signals or barrier semaphores. Data moves between devices by JAX's collectives and lax.ppermute only.
A program may use at most 64 MiB of HBM per device.

v0:
```python
import math

import jax
import jax.numpy as jnp
from jax import lax
from jax.sharding import PartitionSpec as P

HEAD = 64


masked_score = -1e30


def from_behind(value, axis, steps):
    count = lax.axis_size(axis)
    pairs = [(source, (source + steps) % count) for source in range(count)]
    return lax.ppermute(value, axis, pairs)


def head_logits(query_heads, key_rows, allowed, score_scale):
    row_count, head_count, head_size = query_heads.shape
    products = (
        jnp.einsum(
            "qhd,khd->hqk",
            query_heads,
            key_rows.reshape(row_count, head_count, head_size),
            preferred_element_type=jnp.float32,
        )
        * score_scale
    )
    return jnp.where(allowed, products, masked_score)


def on_device(queries, keys, values, out_grad, key_blocks):
    row_count, feature_width = queries.shape
    head_count = feature_width // HEAD
    score_scale = 1.0 / math.sqrt(HEAD)
    reach_count = key_blocks.shape[1]
    live_flags = key_blocks[0] >= 0
    query_heads = queries.reshape(row_count, head_count, HEAD)
    grad_heads = out_grad.reshape(row_count, head_count, HEAD)
    causal_keep = (
        lax.broadcasted_iota(jnp.int32, (row_count, row_count), 1)
        <= lax.broadcasted_iota(jnp.int32, (row_count, row_count), 0)
    )[None]
    own_pair = jnp.stack((keys, values))

    def allowed_at(distance):
        if distance == 0:
            return causal_keep
        return live_flags[distance]

    def fetch_pair(previous):
        return from_behind(previous, "tm", 1)

    carried = (
        jnp.full((head_count, row_count, 1), masked_score, jnp.float32),
        jnp.zeros((head_count, row_count, 1), jnp.float32),
    )
    key_rows = keys
    for distance in range(reach_count):
        if distance > 0:
            key_rows = from_behind(key_rows, "tm", 1)
        running_peak, running_total = carried
        stats_logits = head_logits(query_heads, key_rows, allowed_at(distance), score_scale)
        new_peak = jnp.maximum(running_peak, jnp.max(stats_logits, axis=2, keepdims=True))
        running_total = running_total * jnp.exp(running_peak - new_peak) + jnp.sum(
            jnp.exp(stats_logits - new_peak), axis=2, keepdims=True
        )
        carried = (new_peak, running_total)
    log_total = carried[0] + jnp.log(carried[1])
    output_sum = jnp.zeros((row_count, head_count, HEAD), jnp.float32)
    pair_rows = own_pair
    for distance in range(reach_count):
        if distance > 0:
            pair_rows = fetch_pair(pair_rows)
        output_logits = head_logits(query_heads, pair_rows[0], allowed_at(distance), score_scale)
        output_weights = jnp.exp(output_logits - log_total).astype(jnp.bfloat16)
        output_value_heads = pair_rows[1].reshape(row_count, head_count, HEAD)
        output_sum = output_sum + jnp.einsum(
            "hqk,khd->qhd", output_weights, output_value_heads, preferred_element_type=jnp.float32
        )
    output_heads = output_sum.astype(jnp.bfloat16)
    row_delta = jnp.sum(
        grad_heads.astype(jnp.float32) * output_heads.astype(jnp.float32), axis=2
    ).T[:, :, None]

    def grad_step(pair_rows, distance):
        logits = head_logits(query_heads, pair_rows[0], allowed_at(distance), score_scale)
        weights = jnp.exp(logits - log_total).astype(jnp.bfloat16)
        key_heads = pair_rows[0].reshape(row_count, head_count, HEAD)
        value_heads = pair_rows[1].reshape(row_count, head_count, HEAD)
        prob_grad = jnp.einsum(
            "qhd,khd->hqk", grad_heads, value_heads, preferred_element_type=jnp.float32
        )
        score_grad = (weights.astype(jnp.float32) * (prob_grad - row_delta) * score_scale).astype(
            jnp.bfloat16
        )
        query_part = jnp.einsum(
            "hqk,khd->qhd", score_grad, key_heads, preferred_element_type=jnp.float32
        )
        key_part = jnp.einsum(
            "hqk,qhd->khd", score_grad, query_heads, preferred_element_type=jnp.float32
        ).reshape(row_count, feature_width)
        value_part = jnp.einsum(
            "hqk,qhd->khd", weights, grad_heads, preferred_element_type=jnp.float32
        ).reshape(row_count, feature_width)
        return (query_part, jnp.stack((key_part, value_part)))

    query_grad, pair_grads = grad_step(own_pair, 0)
    pair_rows = own_pair
    for distance in range(1, reach_count):
        pair_rows = fetch_pair(pair_rows)
        query_part, portion = grad_step(pair_rows, distance)
        query_grad = query_grad + query_part
        pair_grads = from_behind(pair_grads, "tm", 1) + portion
    pair_grads = from_behind(pair_grads.astype(jnp.bfloat16), "tm", 1 - reach_count).astype(
        pair_grads.dtype
    )
    return (
        query_grad.reshape(row_count, feature_width).astype(jnp.bfloat16),
        pair_grads[0].astype(jnp.bfloat16),
        pair_grads[1].astype(jnp.bfloat16),
    )


def solution(mesh):
    return jax.shard_map(
        on_device,
        mesh=mesh,
        in_specs=(
            P(("groups", "tm"), None),
            P(("groups", "tm"), None),
            P(("groups", "tm"), None),
            P(("groups", "tm"), None),
            P(("groups", "tm"), None),
        ),
        out_specs=(P(("groups", "tm"), None), P(("groups", "tm"), None), P(("groups", "tm"), None)),
        check_vma=False,
    )
```

profile of v0, /device:TPU:24, one launch (start us, length us, event | category | flops | bytes accessed | tf_op | source)
XLA Modules:
  0.0 147.8 jit_solution(5258373399070478756)
XLA Ops:
  3.5 5.2 %collective-permute-start.5 = (bf16[2,128,256]{2,1,0:T(8,128)(2,1)S(1)}, bf16[2,128,256]{2,1,0:T(8,128)(2,1)S(1)}, u32[]{:S(2)}, u32[]{:S(2)}) collective-permute-start(bf16[2,128,256]{2,1,0:T(8,128)(2,1)S(1)} %pad_maximum_fusion.1), channel_id=1, source_target_pairs={{0,8},{8,16},{16,24},{24,32},{32,40},{40,48},{48,56},{56,64},{64,7... | collective-permute-start | bytes 393224 | tf_op jit(solution)/shard_map/ppermute | solution.py:17
  12.1 4.0 %collective-permute-done = bf16[128,256]{1,0:T(8,128)(2,1)S(1)} collective-permute-done((bf16[128,256]{1,0:T(8,128)(2,1)}, bf16[128,256]{1,0:T(8,128)(2,1)S(1)}, u32[]{:S(2)}, u32[]{:S(2)}) %collective-permute-start) | collective-permute-done | bytes 65568 | tf_op jit(solution)/shard_map/ppermute | solution.py:17
  19.0 6.2 %collective-permute-done.1 = bf16[128,256]{1,0:T(8,128)(2,1)S(1)} collective-permute-done((bf16[128,256]{1,0:T(8,128)(2,1)S(1)}, bf16[128,256]{1,0:T(8,128)(2,1)S(1)}, u32[]{:S(2)}, u32[]{:S(2)}) %collective-permute-start.1) | collective-permute-done | bytes 65568 | tf_op jit(solution)/shard_map/ppermute | solution.py:17
  28.4 1.9 %collective-permute-start.6 = (bf16[2,128,256]{2,1,0:T(8,128)(2,1)S(1)}, bf16[2,128,256]{2,1,0:T(8,128)(2,1)S(1)}, u32[]{:S(2)}, u32[]{:S(2)}) collective-permute-start(bf16[2,128,256]{2,1,0:T(8,128)(2,1)S(1)} %collective-permute-done.5), channel_id=1, source_target_pairs={{0,8},{8,16},{16,24},{24,32},{32,40},{40,48},{48,56},{56,64},{64,7... | collective-permute-start | bytes 393224 | tf_op jit(solution)/shard_map/ppermute | solution.py:17
  30.3 4.1 %collective-permute-done.2 = bf16[128,256]{1,0:T(8,128)(2,1)S(1)} collective-permute-done((bf16[128,256]{1,0:T(8,128)(2,1)S(1)}, bf16[128,256]{1,0:T(8,128)(2,1)S(1)}, u32[]{:S(2)}, u32[]{:S(2)}) %collective-permute-start.2) | collective-permute-done | bytes 65568 | tf_op jit(solution)/shard_map/ppermute | solution.py:17
  37.4 6.2 %collective-permute-done.3 = bf16[128,256]{1,0:T(8,128)(2,1)S(1)} collective-permute-done((bf16[128,256]{1,0:T(8,128)(2,1)S(1)}, bf16[128,256]{1,0:T(8,128)(2,1)S(1)}, u32[]{:S(2)}, u32[]{:S(2)}) %collective-permute-start.3) | collective-permute-done | bytes 65568 | tf_op jit(solution)/shard_map/ppermute | solution.py:17
  46.9 1.9 %collective-permute-start.7 = (bf16[2,128,256]{2,1,0:T(8,128)(2,1)S(1)}, bf16[2,128,256]{2,1,0:T(8,128)(2,1)S(1)}, u32[]{:S(2)}, u32[]{:S(2)}) collective-permute-start(bf16[2,128,256]{2,1,0:T(8,128)(2,1)S(1)} %collective-permute-done.6), channel_id=1, source_target_pairs={{0,8},{8,16},{16,24},{24,32},{32,40},{40,48},{48,56},{56,64},{64,7... | collective-permute-start | bytes 393224 | tf_op jit(solution)/shard_map/ppermute | solution.py:17
  48.8 4.0 %collective-permute-done.4 = bf16[128,256]{1,0:T(8,128)(2,1)S(1)} collective-permute-done((bf16[128,256]{1,0:T(8,128)(2,1)S(1)}, bf16[128,256]{1,0:T(8,128)(2,1)S(1)}, u32[]{:S(2)}, u32[]{:S(2)}) %collective-permute-start.4) | collective-permute-done | bytes 65568 | tf_op jit(solution)/shard_map/ppermute | solution.py:17
  58.9 1.9 %collective-permute-start.8 = (bf16[2,128,256]{2,1,0:T(8,128)(2,1)S(1)}, bf16[2,128,256]{2,1,0:T(8,128)(2,1)S(1)}, u32[]{:S(2)}, u32[]{:S(2)}) collective-permute-start(bf16[2,128,256]{2,1,0:T(8,128)(2,1)S(1)} %collective-permute-done.7), channel_id=1, source_target_pairs={{0,8},{8,16},{16,24},{24,32},{32,40},{40,48},{48,56},{56,64},{64,7... | collective-permute-start | bytes 393224 | tf_op jit(solution)/shard_map/ppermute | solution.py:17
  61.0 7.8 %collective-permute-done.8 = bf16[2,128,256]{2,1,0:T(8,128)(2,1)S(1)} collective-permute-done((bf16[2,128,256]{2,1,0:T(8,128)(2,1)S(1)}, bf16[2,128,256]{2,1,0:T(8,128)(2,1)S(1)}, u32[]{:S(2)}, u32[]{:S(2)}) %collective-permute-start.8) | collective-permute-done | bytes 131104 | tf_op jit(solution)/shard_map/ppermute | solution.py:17
  70.2 1.9 %collective-permute-start.9 = (bf16[2,128,256]{2,1,0:T(8,128)(2,1)S(1)}, bf16[2,128,256]{2,1,0:T(8,128)(2,1)S(1)}, u32[]{:S(2)}, u32[]{:S(2)}) collective-permute-start(bf16[2,128,256]{2,1,0:T(8,128)(2,1)S(1)} %collective-permute-done.8), channel_id=1, source_target_pairs={{0,8},{8,16},{16,24},{24,32},{32,40},{40,48},{48,56},{56,64},{64,7... | collective-permute-start | bytes 393224 | tf_op jit(solution)/shard_map/ppermute | solution.py:17
  72.3 7.8 %collective-permute-done.9 = bf16[2,128,256]{2,1,0:T(8,128)(2,1)S(1)} collective-permute-done((bf16[2,128,256]{2,1,0:T(8,128)(2,1)S(1)}, bf16[2,128,256]{2,1,0:T(8,128)(2,1)S(1)}, u32[]{:S(2)}, u32[]{:S(2)}) %collective-permute-start.9) | collective-permute-done | bytes 131104 | tf_op jit(solution)/shard_map/ppermute | solution.py:17
  83.4 1.9 %collective-permute-start.10 = (f32[2,128,256]{2,1,0:T(8,128)S(1)}, f32[2,128,256]{2,1,0:T(8,128)S(1)}, u32[]{:S(2)}, u32[]{:S(2)}) collective-permute-start(f32[2,128,256]{2,1,0:T(8,128)S(1)} %pad_maximum_fusion), channel_id=1, source_target_pairs={{0,8},{8,16},{16,24},{24,32},{32,40},{40,48},{48,56},{56,64},{64,7... | collective-permute-start | bytes 786440 | tf_op jit(solution)/shard_map/ppermute | solution.py:17
  85.9 8.9 %collective-permute-done.10 = f32[2,128,256]{2,1,0:T(8,128)S(1)} collective-permute-done((f32[2,128,256]{2,1,0:T(8,128)S(1)}, f32[2,128,256]{2,1,0:T(8,128)S(1)}, u32[]{:S(2)}, u32[]{:S(2)}) %collective-permute-start.10) | collective-permute-done | bytes 262176 | tf_op jit(solution)/shard_map/ppermute | solution.py:17
  94.8 1.9 %collective-permute-start.11 = (f32[2,128,256]{2,1,0:T(8,128)S(1)}, f32[2,128,256]{2,1,0:T(8,128)S(1)}, u32[]{:S(2)}, u32[]{:S(2)}) collective-permute-start(f32[2,128,256]{2,1,0:T(8,128)S(1)} %maximum_add_fusion), channel_id=1, source_target_pairs={{0,8},{8,16},{16,24},{24,32},{32,40},{40,48},{48,56},{56,64},{64,7... | collective-permute-start | bytes 786440 | tf_op jit(solution)/shard_map/ppermute | solution.py:17
  97.2 8.9 %collective-permute-done.11 = f32[2,128,256]{2,1,0:T(8,128)S(1)} collective-permute-done((f32[2,128,256]{2,1,0:T(8,128)S(1)}, f32[2,128,256]{2,1,0:T(8,128)S(1)}, u32[]{:S(2)}, u32[]{:S(2)}) %collective-permute-start.11) | collective-permute-done | bytes 262176 | tf_op jit(solution)/shard_map/ppermute | solution.py:17
  106.1 1.9 %collective-permute-start.12 = (f32[2,128,256]{2,1,0:T(8,128)S(1)}, f32[2,128,256]{2,1,0:T(8,128)S(1)}, u32[]{:S(2)}, u32[]{:S(2)}) collective-permute-start(f32[2,128,256]{2,1,0:T(8,128)S(1)} %maximum_add_fusion.1), channel_id=1, source_target_pairs={{0,8},{8,16},{16,24},{24,32},{32,40},{40,48},{48,56},{56,64},{64,7... | collective-permute-start | bytes 786440 | tf_op jit(solution)/shard_map/ppermute | solution.py:17
  108.5 8.9 %collective-permute-done.12 = f32[2,128,256]{2,1,0:T(8,128)S(1)} collective-permute-done((f32[2,128,256]{2,1,0:T(8,128)S(1)}, f32[2,128,256]{2,1,0:T(8,128)S(1)}, u32[]{:S(2)}, u32[]{:S(2)}) %collective-permute-start.12) | collective-permute-done | bytes 262176 | tf_op jit(solution)/shard_map/ppermute | solution.py:17
  117.5 1.9 %collective-permute-start.13 = (f32[2,128,256]{2,1,0:T(8,128)S(1)}, f32[2,128,256]{2,1,0:T(8,128)S(1)}, u32[]{:S(2)}, u32[]{:S(2)}) collective-permute-start(f32[2,128,256]{2,1,0:T(8,128)S(1)} %maximum_add_fusion.2), channel_id=1, source_target_pairs={{0,8},{8,16},{16,24},{24,32},{32,40},{40,48},{48,56},{56,64},{64,7... | collective-permute-start | bytes 786440 | tf_op jit(solution)/shard_map/ppermute | solution.py:17
  119.8 8.9 %collective-permute-done.13 = f32[2,128,256]{2,1,0:T(8,128)S(1)} collective-permute-done((f32[2,128,256]{2,1,0:T(8,128)S(1)}, f32[2,128,256]{2,1,0:T(8,128)S(1)}, u32[]{:S(2)}, u32[]{:S(2)}) %collective-permute-start.13) | collective-permute-done | bytes 262176 | tf_op jit(solution)/shard_map/ppermute | solution.py:17
  128.8 1.9 %collective-permute-start.14 = (f32[2,128,256]{2,1,0:T(8,128)S(1)}, f32[2,128,256]{2,1,0:T(8,128)S(1)}, u32[]{:S(2)}, u32[]{:S(2)}) collective-permute-start(f32[2,128,256]{2,1,0:T(8,128)S(1)} %maximum_add_fusion.3), channel_id=1, source_target_pairs={{0,8},{8,16},{16,24},{24,32},{32,40},{40,48},{48,56},{56,64},{64,7... | collective-permute-start | bytes 786440 | tf_op jit(solution)/shard_map/ppermute | solution.py:17
  131.3 9.2 %collective-permute-done.14 = f32[2,128,256]{2,1,0:T(8,128)S(1)} collective-permute-done((f32[2,128,256]{2,1,0:T(8,128)S(1)}, f32[2,128,256]{2,1,0:T(8,128)S(1)}, u32[]{:S(2)}, u32[]{:S(2)}) %collective-permute-start.14) | collective-permute-done | bytes 262176 | tf_op jit(solution)/shard_map/ppermute | solution.py:17
  140.5 1.9 %collective-permute-start.15 = (bf16[2,128,256]{2,1,0:T(8,128)(2,1)S(1)}, bf16[2,128,256]{2,1,0:T(8,128)(2,1)S(1)}, u32[]{:S(2)}, u32[]{:S(2)}) collective-permute-start(bf16[2,128,256]{2,1,0:T(8,128)(2,1)S(1)} %fusion.59), channel_id=1, source_target_pairs={{0,472},{8,480},{16,488},{24,496},{32,504},{40,0},{48,8},{56,16},{... | collective-permute-start | bytes 393224 | tf_op jit(solution)/shard_map/ppermute | solution.py:17
  143.4 3.7 %collective-permute-done.15 = bf16[2,128,256]{2,1,0:T(8,128)(2,1)S(1)} collective-permute-done((bf16[2,128,256]{2,1,0:T(8,128)(2,1)S(1)}, bf16[2,128,256]{2,1,0:T(8,128)(2,1)S(1)}, u32[]{:S(2)}, u32[]{:S(2)}) %collective-permute-start.15) | collective-permute-done | bytes 131104 | tf_op jit(solution)/shard_map/ppermute | solution.py:17
  (113 shorter events, 33.4 us)
Async XLA Ops:
  0.6 15.5 %collective-permute-start = (bf16[128,256]{1,0:T(8,128)(2,1)}, bf16[128,256]{1,0:T(8,128)(2,1)S(1)}, u32[]{:S(2)}, u32[]{:S(2)}) collective-permute-start(bf16[128,256]{1,0:T(8,128)(2,1)} %param.6), channel_id=1, source_target_pairs={{0,8},{8,16},{16,24},{24,32},{32,40},{40,48},{48,56},{56,64},{64,7... | collective-permute-start | bytes 196616 | tf_op jit(solution)/shard_map/ppermute | solution.py:17
  2.6 6.1 %copy-start.1 = (bf16[128,256]{1,0:T(8,128)(2,1)S(1)}, bf16[128,256]{1,0:T(8,128)(2,1)}, u32[]{:S(2)}) copy-start(bf16[128,256]{1,0:T(8,128)(2,1)} %param.6) | copy-start | bytes 196612
  3.5 5.3 %copy-start = (bf16[128,256]{1,0:T(8,128)(2,1)S(1)}, bf16[128,256]{1,0:T(8,128)(2,1)}, u32[]{:S(2)}) copy-start(bf16[128,256]{1,0:T(8,128)(2,1)} %param.7) | copy-start | bytes 196612
  3.5 24.6 %collective-permute-start.5 = (bf16[2,128,256]{2,1,0:T(8,128)(2,1)S(1)}, bf16[2,128,256]{2,1,0:T(8,128)(2,1)S(1)}, u32[]{:S(2)}, u32[]{:S(2)}) collective-permute-start(bf16[2,128,256]{2,1,0:T(8,128)(2,1)S(1)} %pad_maximum_fusion.1), channel_id=1, source_target_pairs={{0,8},{8,16},{16,24},{24,32},{32,40},{40,48},{48,56},{56,64},{64,7... | collective-permute-start | bytes 393224 | tf_op jit(solution)/shard_map/ppermute | solution.py:17
  8.8 0.8 copy-start.2
  9.7 0.8 copy-start.3
  10.5 0.7 copy-start.4
  16.1 9.2 %collective-permute-start.1 = (bf16[128,256]{1,0:T(8,128)(2,1)S(1)}, bf16[128,256]{1,0:T(8,128)(2,1)S(1)}, u32[]{:S(2)}, u32[]{:S(2)}) collective-permute-start(bf16[128,256]{1,0:T(8,128)(2,1)S(1)} %collective-permute-done), channel_id=1, source_target_pairs={{0,8},{8,16},{16,24},{24,32},{32,40},{40,48},{48,56},{56,64},{64,7... | collective-permute-start | bytes 196616 | tf_op jit(solution)/shard_map/ppermute | solution.py:17
  25.3 9.2 %collective-permute-start.2 = (bf16[128,256]{1,0:T(8,128)(2,1)S(1)}, bf16[128,256]{1,0:T(8,128)(2,1)S(1)}, u32[]{:S(2)}, u32[]{:S(2)}) collective-permute-start(bf16[128,256]{1,0:T(8,128)(2,1)S(1)} %collective-permute-done.1), channel_id=1, source_target_pairs={{0,8},{8,16},{16,24},{24,32},{32,40},{40,48},{48,56},{56,64},{64,7... | collective-permute-start | bytes 196616 | tf_op jit(solution)/shard_map/ppermute | solution.py:17
  28.4 18.2 %collective-permute-start.6 = (bf16[2,128,256]{2,1,0:T(8,128)(2,1)S(1)}, bf16[2,128,256]{2,1,0:T(8,128)(2,1)S(1)}, u32[]{:S(2)}, u32[]{:S(2)}) collective-permute-start(bf16[2,128,256]{2,1,0:T(8,128)(2,1)S(1)} %collective-permute-done.5), channel_id=1, source_target_pairs={{0,8},{8,16},{16,24},{24,32},{32,40},{40,48},{48,56},{56,64},{64,7... | collective-permute-start | bytes 393224 | tf_op jit(solution)/shard_map/ppermute | solution.py:17
  34.5 9.2 %collective-permute-start.3 = (bf16[128,256]{1,0:T(8,128)(2,1)S(1)}, bf16[128,256]{1,0:T(8,128)(2,1)S(1)}, u32[]{:S(2)}, u32[]{:S(2)}) collective-permute-start(bf16[128,256]{1,0:T(8,128)(2,1)S(1)} %collective-permute-done.2), channel_id=1, source_target_pairs={{0,8},{8,16},{16,24},{24,32},{32,40},{40,48},{48,56},{56,64},{64,7... | collective-permute-start | bytes 196616 | tf_op jit(solution)/shard_map/ppermute | solution.py:17
  43.6 9.2 %collective-permute-start.4 = (bf16[128,256]{1,0:T(8,128)(2,1)S(1)}, bf16[128,256]{1,0:T(8,128)(2,1)S(1)}, u32[]{:S(2)}, u32[]{:S(2)}) collective-permute-start(bf16[128,256]{1,0:T(8,128)(2,1)S(1)} %collective-permute-done.3), channel_id=1, source_target_pairs={{0,8},{8,16},{16,24},{24,32},{32,40},{40,48},{48,56},{56,64},{64,7... | collective-permute-start | bytes 196616 | tf_op jit(solution)/shard_map/ppermute | solution.py:17
  46.9 10.5 %collective-permute-start.7 = (bf16[2,128,256]{2,1,0:T(8,128)(2,1)S(1)}, bf16[2,128,256]{2,1,0:T(8,128)(2,1)S(1)}, u32[]{:S(2)}, u32[]{:S(2)}) collective-permute-start(bf16[2,128,256]{2,1,0:T(8,128)(2,1)S(1)} %collective-permute-done.6), channel_id=1, source_target_pairs={{0,8},{8,16},{16,24},{24,32},{32,40},{40,48},{48,56},{56,64},{64,7... | collective-permute-start | bytes 393224 | tf_op jit(solution)/shard_map/ppermute | solution.py:17
  58.9 9.9 %collective-permute-start.8 = (bf16[2,128,256]{2,1,0:T(8,128)(2,1)S(1)}, bf16[2,128,256]{2,1,0:T(8,128)(2,1)S(1)}, u32[]{:S(2)}, u32[]{:S(2)}) collective-permute-start(bf16[2,128,256]{2,1,0:T(8,128)(2,1)S(1)} %collective-permute-done.7), channel_id=1, source_target_pairs={{0,8},{8,16},{16,24},{24,32},{32,40},{40,48},{48,56},{56,64},{64,7... | collective-permute-start | bytes 393224 | tf_op jit(solution)/shard_map/ppermute | solution.py:17
  70.2 9.9 %collective-permute-start.9 = (bf16[2,128,256]{2,1,0:T(8,128)(2,1)S(1)}, bf16[2,128,256]{2,1,0:T(8,128)(2,1)S(1)}, u32[]{:S(2)}, u32[]{:S(2)}) collective-permute-start(bf16[2,128,256]{2,1,0:T(8,128)(2,1)S(1)} %collective-permute-done.8), channel_id=1, source_target_pairs={{0,8},{8,16},{16,24},{24,32},{32,40},{40,48},{48,56},{56,64},{64,7... | collective-permute-start | bytes 393224 | tf_op jit(solution)/shard_map/ppermute | solution.py:17
  83.4 11.3 %collective-permute-start.10 = (f32[2,128,256]{2,1,0:T(8,128)S(1)}, f32[2,128,256]{2,1,0:T(8,128)S(1)}, u32[]{:S(2)}, u32[]{:S(2)}) collective-permute-start(f32[2,128,256]{2,1,0:T(8,128)S(1)} %pad_maximum_fusion), channel_id=1, source_target_pairs={{0,8},{8,16},{16,24},{24,32},{32,40},{40,48},{48,56},{56,64},{64,7... | collective-permute-start | bytes 786440 | tf_op jit(solution)/shard_map/ppermute | solution.py:17
  94.8 11.3 %collective-permute-start.11 = (f32[2,128,256]{2,1,0:T(8,128)S(1)}, f32[2,128,256]{2,1,0:T(8,128)S(1)}, u32[]{:S(2)}, u32[]{:S(2)}) collective-permute-start(f32[2,128,256]{2,1,0:T(8,128)S(1)} %maximum_add_fusion), channel_id=1, source_target_pairs={{0,8},{8,16},{16,24},{24,32},{32,40},{40,48},{48,56},{56,64},{64,7... | collective-permute-start | bytes 786440 | tf_op jit(solution)/shard_map/ppermute | solution.py:17
  106.1 11.3 %collective-permute-start.12 = (f32[2,128,256]{2,1,0:T(8,128)S(1)}, f32[2,128,256]{2,1,0:T(8,128)S(1)}, u32[]{:S(2)}, u32[]{:S(2)}) collective-permute-start(f32[2,128,256]{2,1,0:T(8,128)S(1)} %maximum_add_fusion.1), channel_id=1, source_target_pairs={{0,8},{8,16},{16,24},{24,32},{32,40},{40,48},{48,56},{56,64},{64,7... | collective-permute-start | bytes 786440 | tf_op jit(solution)/shard_map/ppermute | solution.py:17
  117.5 11.3 %collective-permute-start.13 = (f32[2,128,256]{2,1,0:T(8,128)S(1)}, f32[2,128,256]{2,1,0:T(8,128)S(1)}, u32[]{:S(2)}, u32[]{:S(2)}) collective-permute-start(f32[2,128,256]{2,1,0:T(8,128)S(1)} %maximum_add_fusion.2), channel_id=1, source_target_pairs={{0,8},{8,16},{16,24},{24,32},{32,40},{40,48},{48,56},{56,64},{64,7... | collective-permute-start | bytes 786440 | tf_op jit(solution)/shard_map/ppermute | solution.py:17
  128.8 11.7 %collective-permute-start.14 = (f32[2,128,256]{2,1,0:T(8,128)S(1)}, f32[2,128,256]{2,1,0:T(8,128)S(1)}, u32[]{:S(2)}, u32[]{:S(2)}) collective-permute-start(f32[2,128,256]{2,1,0:T(8,128)S(1)} %maximum_add_fusion.3), channel_id=1, source_target_pairs={{0,8},{8,16},{16,24},{24,32},{32,40},{40,48},{48,56},{56,64},{64,7... | collective-permute-start | bytes 786440 | tf_op jit(solution)/shard_map/ppermute | solution.py:17
  140.5 6.6 %collective-permute-start.15 = (bf16[2,128,256]{2,1,0:T(8,128)(2,1)S(1)}, bf16[2,128,256]{2,1,0:T(8,128)(2,1)S(1)}, u32[]{:S(2)}, u32[]{:S(2)}) collective-permute-start(bf16[2,128,256]{2,1,0:T(8,128)(2,1)S(1)} %fusion.59), channel_id=1, source_target_pairs={{0,472},{8,480},{16,488},{24,496},{32,504},{40,0},{48,8},{56,16},{... | collective-permute-start | bytes 393224 | tf_op jit(solution)/shard_map/ppermute | solution.py:17
where the time goes:
time: 149 us; the launch traced here: 148 us
  waiting for transfers between devices  88.8 us (60%)
  starting transfers between devices  33.9 us (23%)
  matrix products  14.7 us (10%)
  local copies, waits for them, and re-layouts  7.59 us (5%)
  other arithmetic  1.51 us (1%)
    ppermute x16, waiting for transfers between devices, from_behind(): return lax.ppermute(value, axis, pairs)  88.8 us
    ppermute x16, starting transfers between devices, from_behind(): return lax.ppermute(value, axis, pairs)  33.9 us
    dot_general x11, matrix products, head_logits(): jnp.einsum('qhd,khd->hqk', query_heads, key_rows.reshape(row_count, head_...  9.2 us
    unnamed x15, local copies, waits for them, and re-layouts  3.16 us
  transfers between devices with their start and end apart: 16, of which 13 were waited for; matrix products, arithmetic and copies ran while one was open for 10% of the time, Pallas kernels for 0%

commit v1 on v0

v1 whole, which is shorter than its diff:
```python
import math

import jax
import jax.numpy as jnp
from jax import lax
from jax.experimental import pallas as pl
from jax.experimental.pallas import tpu as pltpu
from jax.sharding import PartitionSpec as P

HEAD = 64
ROWS = 128
HALF = 128
REACH = 6
FLAGS = 16
MESSAGE = 4 * ROWS + FLAGS
MASKED = -1e30

VMEM = pl.BlockSpec(memory_space=pltpu.VMEM)
SMEM = pl.BlockSpec(memory_space=pltpu.SMEM)


def pack_kernel(blocks_ref, q_ref, k_ref, v_ref, g_ref, out_ref):
    out_ref[0:ROWS, :] = k_ref[...]
    out_ref[ROWS : 2 * ROWS, :] = v_ref[...]
    out_ref[2 * ROWS : 3 * ROWS, :] = q_ref[...]
    out_ref[3 * ROWS : 4 * ROWS, :] = g_ref[...]
    row = lax.broadcasted_iota(jnp.int32, (FLAGS, 2 * HALF), 0)
    flags = jnp.zeros((FLAGS, 2 * HALF), jnp.float32)
    for distance in range(REACH):
        live = (blocks_ref[0, distance] >= 0).astype(jnp.float32)
        flags = jnp.where(row == distance, live, flags)
    out_ref[4 * ROWS :, :] = flags.astype(jnp.bfloat16)


def by_head(rows):
    lane = lax.broadcasted_iota(jnp.int32, rows.shape, 1)
    zero = jnp.zeros_like(rows)
    return jnp.concatenate(
        [jnp.where(lane < HEAD, rows, zero), jnp.where(lane >= HEAD, rows, zero)], axis=0
    )


def grad_kernel(
    core_ref, pair_ref, ahead_ref, behind_ref, far_ref, ahead_got, behind_got, far_got,
    out_ref, keys, values, queries, grads, flags,
):
    core = core_ref[0]

    def put_key(slot, source, start, columns):
        rows = slice(slot * ROWS, (slot + 1) * ROWS)
        keys[rows, :] = source[start : start + ROWS, columns]
        values[rows, :] = source[start + ROWS : start + 2 * ROWS, columns]

    def put_query(slot, source, start, columns):
        rows = slice(slot * ROWS, (slot + 1) * ROWS)
        queries[rows, :] = source[start + 2 * ROWS : start + 3 * ROWS, columns]
        grads[rows, :] = source[start + 3 * ROWS : start + 4 * ROWS, columns]
        flags[slot * FLAGS : (slot + 1) * FLAGS, :] = source[
            start + 4 * ROWS : start + MESSAGE, columns
        ]

    for mine in range(2):

        @pl.when(core == mine)
        def _(mine=mine):
            own = slice(mine * HALF, (mine + 1) * HALF)
            every = slice(0, HALF)
            if mine == 0:
                next1, prev1, on3 = (ahead_ref, own), (behind_ref, own), (far_ref, own)
                next2, prev2, back3 = (ahead_got.at[1], every), (behind_got.at[1], every), (far_got.at[1], every)
            else:
                next1, prev1, on3 = (ahead_got.at[0], every), (behind_got.at[0], every), (far_got.at[0], every)
                next2, prev2, back3 = (ahead_ref, own), (behind_ref, own), (far_ref, own)
            put_key(0, back3[0], 0, back3[1])
            for block in range(2):
                put_key(1 + block, prev2[0], block * 2 * ROWS, prev2[1])
                put_key(3 + block, prev1[0], block * 2 * ROWS, prev1[1])
                put_key(5 + block, pair_ref, block * MESSAGE, own)
                put_key(7 + block, next1[0], block * MESSAGE, next1[1])
                put_key(9 + block, next2[0], block * MESSAGE, next2[1])
                put_query(block, pair_ref, block * MESSAGE, own)
                put_query(2 + block, next1[0], block * MESSAGE, next1[1])
                put_query(4 + block, next2[0], block * MESSAGE, next2[1])
            put_key(11, on3[0], 0, on3[1])
            put_query(6, on3[0], 0, on3[1])

    scale = 1.0 / math.sqrt(HEAD)
    to_base2 = scale * math.log2(math.e)
    both = (((1,), (1,)), ((), ()))
    key_row = lax.broadcasted_iota(jnp.int32, (ROWS, 2 * ROWS), 0)
    query_row = lax.broadcasted_iota(jnp.int32, (ROWS, 2 * ROWS), 1) & (ROWS - 1)
    causal = key_row <= query_row
    lane = lax.broadcasted_iota(jnp.int32, (ROWS, HALF), 1)
    key_grad = [jnp.zeros((ROWS, HALF), jnp.float32) for _ in range(2)]
    value_grad = [jnp.zeros((ROWS, HALF), jnp.float32) for _ in range(2)]

    for slot in range(7):
        rows = slice(slot * ROWS, (slot + 1) * ROWS)
        strip = slice(slot * ROWS, (slot + REACH) * ROWS)
        query_heads = by_head(queries[rows, :])
        grad_heads = by_head(grads[rows, :])
        live = flags[slot * FLAGS : (slot + 1) * FLAGS, :].astype(jnp.float32)
        live = jnp.concatenate([live, live], axis=1)
        strip_keys = keys[strip, :]
        scores = lax.dot_general(strip_keys, query_heads, both, preferred_element_type=jnp.float32)
        prob_grad = lax.dot_general(
            values[strip, :], grad_heads, both, preferred_element_type=jnp.float32
        )
        pieces = [scores[p * ROWS : (p + 1) * ROWS] for p in range(REACH)]
        pieces[0] = jnp.where(live[5:6, :] > 0.0, pieces[0], MASKED)
        pieces[1] = jnp.where(live[4:5, :] > 0.0, pieces[1], MASKED)
        pieces[5] = jnp.where(causal, pieces[5], MASKED)
        grad_pieces = [prob_grad[p * ROWS : (p + 1) * ROWS] for p in range(REACH)]
        peak = pieces[0]
        for piece in pieces[1:]:
            peak = jnp.maximum(peak, piece)
        peak = jnp.max(peak, axis=0, keepdims=True)
        powers = [jnp.exp2((piece - peak) * to_base2) for piece in pieces]
        total = powers[0]
        weighted = powers[0] * grad_pieces[0]
        for power, grad_piece in zip(powers[1:], grad_pieces[1:]):
            total = total + power
            weighted = weighted + power * grad_piece
        inverse = 1.0 / jnp.sum(total, axis=0, keepdims=True)
        row_delta = jnp.sum(weighted, axis=0, keepdims=True) * inverse

        def weights_at(p):
            return (powers[p] * inverse).astype(jnp.bfloat16)

        def score_grad_at(p, weights):
            return (
                weights.astype(jnp.float32) * ((grad_pieces[p] - row_delta) * scale)
            ).astype(jnp.bfloat16)

        needed = range(REACH) if slot < 2 else [p for p in (5 - slot, 6 - slot) if p >= 0]
        weights = {p: weights_at(p) for p in needed}
        score_grads = {p: score_grad_at(p, weights[p]) for p in needed}
        for block in range(2):
            p = 5 + block - slot
            if 0 <= p < REACH:
                key_grad[block] = key_grad[block] + jnp.dot(
                    score_grads[p], query_heads, preferred_element_type=jnp.float32
                )
                value_grad[block] = value_grad[block] + jnp.dot(
                    weights[p], grad_heads, preferred_element_type=jnp.float32
                )
        if slot < 2:
            full = lax.dot_general(
                jnp.concatenate([score_grads[p] for p in range(REACH)], axis=0),
                strip_keys,
                (((0,), (0,)), ((), ())),
                preferred_element_type=jnp.float32,
            )
            query_grad = jnp.where(lane < HEAD, full[:ROWS], full[ROWS:])
            out_ref[slot * 3 * ROWS : (slot * 3 + 1) * ROWS, :] = query_grad.astype(jnp.bfloat16)
    for block in range(2):
        start = block * 3 * ROWS
        out_ref[start + ROWS : start + 2 * ROWS, :] = key_grad[block].astype(jnp.bfloat16)
        out_ref[start + 2 * ROWS : start + 3 * ROWS, :] = value_grad[block].astype(jnp.bfloat16)


def on_device(queries, keys, values, out_grad, key_blocks):
    count = lax.axis_size("tm")
    core = lax.rem(lax.axis_index("tm"), 2)
    cores = [[2 * chip, 2 * chip + 1] for chip in range(count // 2)]

    def send(value, chips_from_core0, chips_from_core1):
        hops = (chips_from_core0, chips_from_core1)
        pairs = [(s, (s + 2 * hops[s % 2]) % count) for s in range(count)]
        return lax.ppermute(value, "tm", pairs)

    def share(value):
        return lax.all_gather(value, "tm", axis_index_groups=cores)

    def swap_halves(value):
        return share(jnp.where(core == 0, value[:, HALF:], value[:, :HALF]))

    own = pl.pallas_call(
        pack_kernel,
        out_shape=jax.ShapeDtypeStruct((MESSAGE, 2 * HALF), jnp.bfloat16),
        in_specs=[SMEM] + [VMEM] * 4,
        out_specs=VMEM,
    )(key_blocks, queries, keys, values, out_grad)
    far = send(own, -3, 3)
    pair = share(own)
    ahead = send(pair.reshape(2 * MESSAGE, 2 * HALF), -1, -2)
    behind = send(pair[:, : 2 * ROWS].reshape(4 * ROWS, 2 * HALF), 1, 2)
    got = swap_halves(jnp.concatenate([behind, far], axis=0))
    behind_got, far_got = got[:, : 4 * ROWS], got[:, 4 * ROWS :]
    ahead_got = swap_halves(ahead)
    result = pl.pallas_call(
        grad_kernel,
        out_shape=jax.ShapeDtypeStruct((6 * ROWS, HALF), jnp.bfloat16),
        in_specs=[SMEM] + [VMEM] * 7,
        out_specs=VMEM,
        scratch_shapes=[
            pltpu.VMEM((12 * ROWS, HALF), jnp.bfloat16),
            pltpu.VMEM((12 * ROWS, HALF), jnp.bfloat16),
            pltpu.VMEM((7 * ROWS, HALF), jnp.bfloat16),
            pltpu.VMEM((7 * ROWS, HALF), jnp.bfloat16),
            pltpu.VMEM((7 * FLAGS, HALF), jnp.bfloat16),
        ],
        compiler_params=pltpu.CompilerParams(vmem_limit_bytes=24 * 1024 * 1024),
    )(
        core.reshape(1), pair.reshape(2 * MESSAGE, 2 * HALF), ahead, behind, far,
        ahead_got, behind_got, far_got,
    )
    both = share(result)
    mine = lax.dynamic_slice(both, (0, core * 3 * ROWS, 0), (2, 3 * ROWS, HALF))
    mine = jnp.concatenate([mine[0], mine[1]], axis=1)
    return mine[:ROWS], mine[ROWS : 2 * ROWS], mine[2 * ROWS :]


def solution(mesh):
    rows = P(("groups", "tm"), None)
    return jax.shard_map(
        on_device,
        mesh=mesh,
        in_specs=(rows,) * 5,
        out_specs=(rows,) * 3,
        check_vma=False,
    )
```

time: 149 us -> 49.3 us (0.33)
  the two profiles are of different devices: /device:TPU:24 before, /device:TPU:1 now
where the time goes in v1:
time: 49.3 us; the launch traced here: 49 us
  blocking collectives  20.4 us (41%)
  waiting for transfers between devices  10.5 us (21%)
  starting transfers between devices  9.72 us (20%)
  Pallas kernels  6.75 us (14%)
  other arithmetic  0.76 us (2%)
  between operations  0.74 us (2%)
    all_gather x4, blocking collectives, share(): return lax.all_gather(value, 'tm', axis_index_groups=cores)  20.4 us
    ppermute x3, waiting for transfers between devices, send(): return lax.ppermute(value, 'tm', pairs)  10.5 us
    ppermute x3, starting transfers between devices, send(): return lax.ppermute(value, 'tm', pairs)  9.72 us
    pallas_call x1, Pallas kernels, on_device(): pl.pallas_call(grad_kernel, out_shape=jax.ShapeDtypeStruct((6 * ROWS, HAL...  5.09 us
    pallas_call x1, Pallas kernels, on_device(): pl.pallas_call(pack_kernel, out_shape=jax.ShapeDtypeStruct((MESSAGE, 2 *...  1.66 us
  transfers between devices with their start and end apart: 3, of which 2 were waited for; matrix products, arithmetic and copies ran while one was open for 0% of the time, Pallas kernels for 0%

profile of v1, /device:TPU:1, one launch (start us, length us, event | category | flops | bytes accessed | tf_op | source)
XLA Modules:
  0.0 49.0 jit_solution(16297795826954123013)
XLA Ops:
  0.6 1.7 %shard_map.76 = bf16[528,256]{1,0:T(8,128)(2,1)} custom-call(s32[1,6]{1,0:T(1,128)} %blocks_ref.1, bf16[128,256]{1,0:T(8,128)(2,1)} %q_ref.1, bf16[128,256]{1,0:T(8,128)(2,1)} %k_ref.1, bf16[128,256]{1,0:T(8,128)(2,1)} %v_ref.1, bf16[128,256]{1,0:T(8,128)(2,1)} %g_ref.1), custom_call_target="tpu_custom_call" | custom-call | tf_op jit(solution)/shard_map/pallas_call | solution.py:178
  2.3 8.9 %all-gather.pair_ref = bf16[1056,256]{1,0:T(8,128)(2,1)S(1)} all-gather(bf16[528,256]{1,0:T(8,128)(2,1)} %shard_map.76), channel_id=2, replica_groups={{0,8},{16,24},{32,40},{48,56},{64,72},{80,88},{96,104},{112,120},{128,1..., dimensions={0}, use_global_device_ids=true | all-gather | bytes 811008 | tf_op jit(solution)/shard_map/all_gather | solution.py:173
  11.2 0.0 copy-start
  11.2 2.1 %collective-permute-start.1 = (bf16[512,256]{1,0:T(8,128)(2,1)S(1)}, bf16[512,256]{1,0:T(8,128)(2,1)S(1)}, u32[]{:S(2)}, u32[]{:S(2)}) collective-permute-start(bf16[512,256]{1,0:T(8,128)(2,1)S(1)} %bitcast.15), channel_id=1, source_target_pairs={{0,16},{8,40},{16,32},{24,56},{32,48},{40,72},{48,64},{56,88},{64,... | collective-permute-start | bytes 786440 | tf_op jit(solution)/shard_map/ppermute | solution.py:170
  13.3 0.0 copy-done
  13.3 2.3 %collective-permute-start.2 = (bf16[528,256]{1,0:T(8,128)(2,1)S(1)}, bf16[528,256]{1,0:T(8,128)(2,1)S(1)}, u32[]{:S(2)}, u32[]{:S(2)}) collective-permute-start(bf16[528,256]{1,0:T(8,128)(2,1)S(1)} %copy-done), channel_id=1, source_target_pairs={{0,464},{8,56},{16,480},{24,72},{32,496},{40,88},{48,0},{56,104},{... | collective-permute-start | bytes 811016 | tf_op jit(solution)/shard_map/ppermute | solution.py:170
  15.5 5.4 %collective-permute-start = (bf16[1056,256]{1,0:T(8,128)(2,1)S(1)}, bf16[1056,256]{1,0:T(8,128)(2,1)S(1)}, u32[]{:S(2)}, u32[]{:S(2)}) collective-permute-start(bf16[1056,256]{1,0:T(8,128)(2,1)S(1)} %all-gather.pair_ref), channel_id=1, source_target_pairs={{0,496},{8,488},{16,0},{24,504},{32,16},{40,8},{48,32},{56,24},{64... | collective-permute-start | bytes 1622024 | tf_op jit(solution)/shard_map/ppermute | solution.py:170
  21.0 0.2 collective-permute-done.1.behind_ref
  21.2 10.3 %collective-permute-done.2.far_ref = bf16[528,256]{1,0:T(8,128)(2,1)S(1)} collective-permute-done((bf16[528,256]{1,0:T(8,128)(2,1)S(1)}, bf16[528,256]{1,0:T(8,128)(2,1)S(1)}, u32[]{:S(2)}, u32[]{:S(2)}) %collective-permute-start.2) | collective-permute-done | bytes 270368 | tf_op jit(solution)/shard_map/ppermute | solution.py:170
  31.6 3.5 %all-gather.2 = bf16[2080,128]{1,0:T(8,128)(2,1)S(1)} all-gather(bf16[1040,128]{1,0:T(8,128)(2,1)S(1)} %slice_select_fusion.1), channel_id=4, replica_groups={{0,8},{16,24},{32,40},{48,56},{64,72},{80,88},{96,104},{112,120},{128,1..., dimensions={0}, use_global_device_ids=true | all-gather | bytes 798720 | tf_op jit(solution)/shard_map/all_gather | solution.py:173
  35.1 0.0 collective-permute-done.ahead_ref
  35.1 6.0 %all-gather.1 = bf16[2112,128]{1,0:T(8,128)(2,1)S(1)} all-gather(bf16[1056,128]{1,0:T(8,128)(2,1)S(1)} %slice_select_fusion), channel_id=3, replica_groups={{0,8},{16,24},{32,40},{48,56},{64,72},{80,88},{96,104},{112,120},{128,1..., dimensions={0}, use_global_device_ids=true | all-gather | bytes 811008 | tf_op jit(solution)/shard_map/all_gather | solution.py:173
  41.1 5.1 %shard_map.77 = bf16[768,128]{1,0:T(8,128)(2,1)S(1)} custom-call(s32[1]{0:T(128)} %bitcast.core_ref, bf16[1056,256]{1,0:T(8,128)(2,1)S(1)} %all-gather.pair_ref, bf16[1056,256]{1,0:T(8,128)(2,1)S(1)} %collective-permute-done.ahead_ref, bf16[512,256]{1,0:T(8,128)(2,1)S(1)} %collective-permute-done.1.behind_ref, ...), custom_call_target="tpu_custom_call" | custom-call | tf_op jit(solution)/shard_map/pallas_call | solution.py:191
  46.2 2.1 %all-gather.3 = bf16[1536,128]{1,0:T(8,128)(2,1)S(1)} all-gather(bf16[768,128]{1,0:T(8,128)(2,1)S(1)} %shard_map.77), channel_id=5, replica_groups={{0,8},{16,24},{32,40},{48,56},{64,72},{80,88},{96,104},{112,120},{128,1..., dimensions={0}, use_global_device_ids=true | all-gather | bytes 589824 | tf_op jit(solution)/shard_map/all_gather | solution.py:173
  48.3 0.7 %pad_maximum_fusion = (bf16[128,256]{1,0:T(8,128)(2,1)}, bf16[128,256]{1,0:T(8,128)(2,1)}, bf16[128,256]{1,0:T(8,128)(2,1)}) fusion(bf16[384,128]{1,0:T(8,128)(2,1)S(1)} %get-tuple-element.3, bf16[384,128]{1,0:T(8,128)(2,1)S(1)} %get-tuple-element.4), kind=kLoop, calls=%fused_computation.10 | loop fusion | flops 393216 | bytes 393216 | tf_op jit(solution)/shard_map/concatenate | solution.py:210
  (8 shorter events, 0.2 us)
Async XLA Ops:
  11.2 2.1 %copy-start = (bf16[528,256]{1,0:T(8,128)(2,1)S(1)}, bf16[528,256]{1,0:T(8,128)(2,1)}, u32[]{:S(2)}) copy-start(bf16[528,256]{1,0:T(8,128)(2,1)} %shard_map.76) | copy-start | bytes 811012
  11.2 9.9 %collective-permute-start.1 = (bf16[512,256]{1,0:T(8,128)(2,1)S(1)}, bf16[512,256]{1,0:T(8,128)(2,1)S(1)}, u32[]{:S(2)}, u32[]{:S(2)}) collective-permute-start(bf16[512,256]{1,0:T(8,128)(2,1)S(1)} %bitcast.15), channel_id=1, source_target_pairs={{0,16},{8,40},{16,32},{24,56},{32,48},{40,72},{48,64},{56,88},{64,... | collective-permute-start | bytes 786440 | tf_op jit(solution)/shard_map/ppermute | solution.py:170
  13.3 18.2 %collective-permute-start.2 = (bf16[528,256]{1,0:T(8,128)(2,1)S(1)}, bf16[528,256]{1,0:T(8,128)(2,1)S(1)}, u32[]{:S(2)}, u32[]{:S(2)}) collective-permute-start(bf16[528,256]{1,0:T(8,128)(2,1)S(1)} %copy-done), channel_id=1, source_target_pairs={{0,464},{8,56},{16,480},{24,72},{32,496},{40,88},{48,0},{56,104},{... | collective-permute-start | bytes 811016 | tf_op jit(solution)/shard_map/ppermute | solution.py:170
  15.5 19.5 %collective-permute-start = (bf16[1056,256]{1,0:T(8,128)(2,1)S(1)}, bf16[1056,256]{1,0:T(8,128)(2,1)S(1)}, u32[]{:S(2)}, u32[]{:S(2)}) collective-permute-start(bf16[1056,256]{1,0:T(8,128)(2,1)S(1)} %all-gather.pair_ref), channel_id=1, source_target_pairs={{0,496},{8,488},{16,0},{24,504},{32,16},{40,8},{48,32},{56,24},{64... | collective-permute-start | bytes 1622024 | tf_op jit(solution)/shard_map/ppermute | solution.py:170

commit v2 on v1

v2 whole, which is shorter than its diff:
```python
import math

import jax
import jax.numpy as jnp
from jax import lax
from jax.experimental import pallas as pl
from jax.experimental.pallas import tpu as pltpu
from jax.sharding import PartitionSpec as P

HEAD = 64
ROWS = 128
HALF = 128
REACH = 6
FLAGS = 16
MESSAGE = 4 * ROWS + FLAGS
MASKED = -1e30
GRANT = 16 * 1024 * 1024

VMEM = pl.BlockSpec(memory_space=pltpu.VMEM)
SMEM = pl.BlockSpec(memory_space=pltpu.SMEM)


def pack_kernel(blocks_ref, q_ref, k_ref, v_ref, g_ref, out_ref, pair_ref):
    for ref, start in ((k_ref, 0), (v_ref, ROWS)):
        rows = ref[...]
        out_ref[start : start + ROWS, :] = rows
        pair_ref[start : start + ROWS, :] = rows
    out_ref[2 * ROWS : 3 * ROWS, :] = q_ref[...]
    out_ref[3 * ROWS : 4 * ROWS, :] = g_ref[...]
    row = lax.broadcasted_iota(jnp.int32, (FLAGS, 2 * HALF), 0)
    flags = jnp.zeros((FLAGS, 2 * HALF), jnp.float32)
    for distance in range(REACH):
        live = (blocks_ref[0, distance] >= 0).astype(jnp.float32)
        flags = jnp.where(row == distance, live, flags)
    out_ref[4 * ROWS :, :] = flags.astype(jnp.bfloat16)


def by_head(rows):
    lane = lax.broadcasted_iota(jnp.int32, rows.shape, 1)
    zero = jnp.zeros_like(rows)
    return jnp.concatenate(
        [jnp.where(lane < HEAD, rows, zero), jnp.where(lane >= HEAD, rows, zero)], axis=0
    )


def take(source, start, count, columns, target, at):
    target[at * ROWS : (at + count) * ROWS, :] = source[start : start + count * ROWS, columns]


def on_core(core, place):
    own = (slice(0, HALF), slice(HALF, 2 * HALF))
    for mine in range(2):

        @pl.when(core == mine)
        def _(mine=mine):
            place(mine, own[mine])


def query_step(strip_keys, strip_values, query_rows, grad_rows, live, needed):
    scale = 1.0 / math.sqrt(HEAD)
    to_base2 = scale * math.log2(math.e)
    both = (((1,), (1,)), ((), ()))
    key_row = lax.broadcasted_iota(jnp.int32, (ROWS, 2 * ROWS), 0)
    query_row = lax.broadcasted_iota(jnp.int32, (ROWS, 2 * ROWS), 1) & (ROWS - 1)
    query_heads = by_head(query_rows)
    grad_heads = by_head(grad_rows)
    live = live.astype(jnp.float32)
    live = jnp.concatenate([live, live], axis=1)
    scores = lax.dot_general(strip_keys, query_heads, both, preferred_element_type=jnp.float32)
    prob_grad = lax.dot_general(
        strip_values, grad_heads, both, preferred_element_type=jnp.float32
    )
    pieces = [scores[p * ROWS : (p + 1) * ROWS] for p in range(REACH)]
    pieces[0] = jnp.where(live[5:6, :] > 0.0, pieces[0], MASKED)
    pieces[1] = jnp.where(live[4:5, :] > 0.0, pieces[1], MASKED)
    pieces[5] = jnp.where(key_row <= query_row, pieces[5], MASKED)
    grad_pieces = [prob_grad[p * ROWS : (p + 1) * ROWS] for p in range(REACH)]
    peak = pieces[0]
    for piece in pieces[1:]:
        peak = jnp.maximum(peak, piece)
    peak = jnp.max(peak, axis=0, keepdims=True)
    powers = [jnp.exp2((piece - peak) * to_base2) for piece in pieces]
    total = powers[0]
    weighted = powers[0] * grad_pieces[0]
    for power, grad_piece in zip(powers[1:], grad_pieces[1:]):
        total = total + power
        weighted = weighted + power * grad_piece
    inverse = 1.0 / jnp.sum(total, axis=0, keepdims=True)
    row_delta = jnp.sum(weighted, axis=0, keepdims=True) * inverse
    weights, score_grads = {}, {}
    for p in needed:
        weights[p] = (powers[p] * inverse).astype(jnp.bfloat16)
        score_grads[p] = (
            weights[p].astype(jnp.float32) * ((grad_pieces[p] - row_delta) * scale)
        ).astype(jnp.bfloat16)
    return query_heads, grad_heads, weights, score_grads


def dots(step, p, sums, key):
    query_heads, grad_heads, weights, score_grads = step
    parts = (
        jnp.dot(score_grads[p], query_heads, preferred_element_type=jnp.float32),
        jnp.dot(weights[p], grad_heads, preferred_element_type=jnp.float32),
    )
    sums[key] = parts if key not in sums else tuple(s + part for s, part in zip(sums[key], parts))


def query_part(strip_keys, score_grads):
    full = lax.dot_general(
        jnp.concatenate([score_grads[p] for p in range(REACH)], axis=0),
        strip_keys,
        (((0,), (0,)), ((), ())),
        preferred_element_type=jnp.float32,
    )
    lane = lax.broadcasted_iota(jnp.int32, (ROWS, HALF), 1)
    return jnp.where(lane < HEAD, full[:ROWS], full[ROWS:]).astype(jnp.bfloat16)


def block_of(ref, index):
    start = index * MESSAGE
    parts = [ref[start + i * ROWS : start + (i + 1) * ROWS, :] for i in range(4)]
    return (*parts, ref[start + 4 * ROWS : start + MESSAGE, :])


def write_sums(ref, sums, first):
    for block in range(2):
        for which in range(2):
            start = (2 * block + which) * ROWS
            ref[start : start + ROWS, :] = sums[first + block][which].astype(ref.dtype)


def read_sums(ref, first):
    return {
        first + block: tuple(
            ref[(2 * block + w) * ROWS : (2 * block + w + 1) * ROWS, :].astype(jnp.float32) for w in range(2)
        )
        for block in range(2)
    }


def own_kernel(
    core_ref, own_ref, behind_ref, far_ref, got_ref,
    keys, values, query_grad, own_sums, back_sums,
):
    every = slice(0, HALF)

    def place(mine, own):
        if mine == 0:
            near, next_, last = (behind_ref, own, 0), (got_ref.at[1], every, 0), (got_ref.at[1], every, 4 * ROWS)
        else:
            near, next_, last = (got_ref.at[0], every, 0), (behind_ref, own, 0), (far_ref, own, 0)
        for (ref, columns, start), first, count in ((last, 0, 1), (next_, 1, 2), (near, 3, 2)):
            for block in range(count):
                take(ref, start + block * 2 * ROWS, 1, columns, keys, first + block)
                take(ref, start + block * 2 * ROWS + ROWS, 1, columns, values, first + block)

    on_core(core_ref[0], place)
    blocks = [block_of(own_ref, block) for block in range(2)]
    for block in range(2):
        rows = slice((5 + block) * ROWS, (6 + block) * ROWS)
        keys[rows, :] = blocks[block][0]
        values[rows, :] = blocks[block][1]
    sums = {}
    for slot in range(2):
        strip = slice(slot * ROWS, (slot + REACH) * ROWS)
        strip_keys = keys[strip, :]
        step = query_step(strip_keys, values[strip, :], *blocks[slot][2:], list(range(REACH)))
        for p in range(REACH):
            if slot + p not in (0, 3, 4):
                dots(step, p, sums, slot + p)
        query_grad[slot * ROWS : (slot + 1) * ROWS, :] = query_part(strip_keys, step[3])
    write_sums(own_sums, sums, 5)
    write_sums(back_sums, sums, 1)


def ahead_step(slot, first, ahead_ref, keys, values, needed, sums):
    strip = slice((slot - first) * ROWS, (slot - first + REACH) * ROWS)
    step = query_step(keys[strip, :], values[strip, :], *block_of(ahead_ref, slot - 2)[2:], needed)
    for p in needed:
        dots(step, p, sums, slot + p)


def ahead_kernel(ahead_ref, keys7, values7, own_in, back_in, own_out, back_out, keys, values):
    for target, source, part in ((keys, keys7, 0), (values, values7, 1)):
        target[: 5 * ROWS, :] = source[2 * ROWS :, :]
        target[5 * ROWS :, :] = block_of(ahead_ref, 0)[part]
    sums = read_sums(own_in, 5) | read_sums(back_in, 1)
    ahead_step(2, 2, ahead_ref, keys, values, [0, 3, 4], sums)
    write_sums(own_out, sums, 5)
    write_sums(back_out, sums, 1)


def after_kernel(ahead_ref, keys7, values7, own_in, own_out, keys, values):
    for target, source, part in ((keys, keys7, 0), (values, values7, 1)):
        target[: 4 * ROWS, :] = source[3 * ROWS :, :]
        for block in range(2):
            target[(4 + block) * ROWS : (5 + block) * ROWS, :] = block_of(ahead_ref, block)[part]
    sums = read_sums(own_in, 5)
    ahead_step(3, 3, ahead_ref, keys, values, [2, 3], sums)
    write_sums(own_out, sums, 5)


def total_of(sums_ref, back_ref, block, which):
    rows = slice((2 * block + which) * ROWS, (2 * block + which + 1) * ROWS)
    return (sums_ref[rows, :] + back_ref[rows, :].astype(jnp.float32)).astype(jnp.bfloat16)


def swap_kernel(core_ref, query_grad, sums_ref, back_ref, out_ref):
    def place(mine, own):
        del own
        other = 1 - mine
        out_ref[:ROWS, :] = query_grad[other * ROWS : (other + 1) * ROWS, :]
        for which in range(2):
            out_ref[(1 + which) * ROWS : (2 + which) * ROWS, :] = total_of(sums_ref, back_ref, other, which)

    on_core(core_ref[0], place)


def last_kernel(core_ref, query_grad, sums_ref, back_ref, got_ref, out_q, out_k, out_v):
    def place(mine, own):
        other = slice((1 - mine) * HALF, (2 - mine) * HALF)
        out_q[:, own] = query_grad[mine * ROWS : (mine + 1) * ROWS, :]
        for which, out in ((0, out_k), (1, out_v)):
            out[:, own] = total_of(sums_ref, back_ref, mine, which)
        for at, out in enumerate((out_q, out_k, out_v)):
            out[:, other] = got_ref[1 - mine, at * ROWS : (at + 1) * ROWS, :]

    on_core(core_ref[0], place)


def call(kernel, name, outs, operands, scratch=(), work=0, scalar=True, grant=GRANT):
    outs = [jax.ShapeDtypeStruct(shape, dtype) for shape, dtype in outs]
    return pl.pallas_call(
        kernel,
        name=name,
        out_shape=outs,
        in_specs=[SMEM] * scalar + [VMEM] * (len(operands) - scalar),
        out_specs=[VMEM] * len(outs),
        scratch_shapes=[pltpu.VMEM((rows, HALF), jnp.bfloat16) for rows in scratch],
        cost_estimate=pl.CostEstimate(
            flops=work * 4 * 768 * 128 * 256, bytes_accessed=work * 1_000_000, transcendentals=work * 768 * 256
        ),
        compiler_params=pltpu.CompilerParams(vmem_limit_bytes=grant),
    )(*operands)


def on_device(queries, keys, values, out_grad, key_blocks):
    bf16, f32 = jnp.bfloat16, jnp.float32
    count = lax.axis_size("tm")
    core = lax.rem(lax.axis_index("tm"), 2)
    which = core.reshape(1)
    cores = [[2 * chip, 2 * chip + 1] for chip in range(count // 2)]

    def send(value, chips_from_core0, chips_from_core1):
        hops = (chips_from_core0, chips_from_core1)
        pairs = [(s, (s + 2 * hops[s % 2]) % count) for s in range(count) if hops[s % 2]]
        return lax.ppermute(value, "tm", pairs)

    def share(value):
        return lax.all_gather(value, "tm", axis_index_groups=cores)

    def half(value, other):
        return jnp.where((core == 0) != other, value[:, :HALF], value[:, HALF:])

    own, own_pair = pl.pallas_call(
        pack_kernel,
        name="pack",
        out_shape=[
            jax.ShapeDtypeStruct((MESSAGE, 2 * HALF), bf16),
            jax.ShapeDtypeStruct((2 * ROWS, 2 * HALF), bf16),
        ],
        in_specs=[SMEM] + [VMEM] * 4,
        out_specs=[VMEM] * 2,
    )(key_blocks, queries, keys, values, out_grad)
    far = send(own_pair, 0, 3)
    pair = share(own)
    behind = send(pair[:, : 2 * ROWS].reshape(4 * ROWS, 2 * HALF), 1, 2)
    ours = half(pair.reshape(2 * MESSAGE, 2 * HALF), False)
    ahead = send(ours, -1, -1)
    got = share(half(jnp.concatenate([behind, far], axis=0), True))
    seven, sums_of = ((7 * ROWS, HALF), bf16), (4 * ROWS, HALF)
    keys7, values7, query_grad, sums, back = call(
        own_kernel, "own", [seven, seven, ((2 * ROWS, HALF), bf16), (sums_of, f32), (sums_of, f32)],
        (which, ours, behind, far, got), work=2,
    )
    sums, back = call(
        ahead_kernel, "ahead", [(sums_of, f32), (sums_of, bf16)], (ahead, keys7, values7, sums, back),
        (6 * ROWS, 6 * ROWS), work=1, scalar=False,
    )
    returned = send(back, -2, -2)
    (sums,) = call(
        after_kernel, "after", [(sums_of, f32)], (ahead, keys7, values7, sums), (6 * ROWS, 6 * ROWS),
        work=1, scalar=False,
    )
    (swap,) = call(
        swap_kernel, "swap", [((3 * ROWS, HALF), bf16)], (which, query_grad, sums, returned)
    )
    return tuple(
        call(
            last_kernel, "last", [((ROWS, 2 * HALF), bf16)] * 3,
            (which, query_grad, sums, returned, share(swap)),
        )
    )


def solution(mesh):
    rows = P(("groups", "tm"), None)
    return jax.shard_map(
        on_device,
        mesh=mesh,
        in_specs=(rows,) * 5,
        out_specs=(rows,) * 3,
        check_vma=False,
    )
```

time: 49.3 us -> 44.8 us (0.909)
  blocking collectives: 20.4 us -> 13.5 us
  starting transfers between devices: 9.72 us -> 15.6 us
  waiting for transfers between devices: 10.5 us -> 8.45 us
  other arithmetic: 0.76 us -> 0.07 us
  Pallas kernels: 6.75 us -> 6.13 us
    all_gather x4 -> x3, blocking collectives: 20.4 us -> 13.5 us  [share(): return lax.all_gather(value, 'tm', axis_index_groups=cores)]
    ppermute x3 -> x4, starting transfers between devices: 9.72 us -> 15.6 us  [send(): return lax.ppermute(value, 'tm', pairs)]
    ppermute x3 -> x4, waiting for transfers between devices: 10.5 us -> 8.45 us  [send(): return lax.ppermute(value, 'tm', pairs)]
    concatenate x1 -> x0, other arithmetic: 0.68 us -> none  [on_device(): mine = jnp.concatenate([mine[0], mine[1]], axis=1)]
    pallas_call x2 -> x6, Pallas kernels: 6.75 us -> 6.13 us  [the longest x5 4.43 us: call(): pl.pallas_call(kernel, name=name, out_shape=outs, in_specs=[SMEM] * scala...]
  transfers between devices with their start and end apart: 3 -> 4, of which waited for: 2 -> 2; matrix products, arithmetic and copies ran while one was open for 0% -> 0% of each run, Pallas kernels for 0% -> 6%
where the time goes in v2:
time: 44.8 us; the launch traced here: 44.5 us
  starting transfers between devices  15.6 us (35%)
  blocking collectives  13.5 us (30%)
  waiting for transfers between devices  8.45 us (19%)
  Pallas kernels  6.13 us (14%)
  between operations  0.75 us (2%)
    ppermute x4, starting transfers between devices, send(): return lax.ppermute(value, 'tm', pairs)  15.6 us
    all_gather x3, blocking collectives, share(): return lax.all_gather(value, 'tm', axis_index_groups=cores)  13.5 us
    ppermute x4, waiting for transfers between devices, send(): return lax.ppermute(value, 'tm', pairs)  8.45 us
    pallas_call x5, Pallas kernels, call(): pl.pallas_call(kernel, name=name, out_shape=outs, in_specs=[SMEM] * scala...  4.43 us
    pallas_call x1, Pallas kernels, on_device(): pl.pallas_call(pack_kernel, name='pack', out_shape=[jax.ShapeDtypeStruct(...  1.7 us
  transfers between devices with their start and end apart: 4, of which 2 were waited for; matrix products, arithmetic and copies ran while one was open for 0% of the time, Pallas kernels for 6%

profile of v2, /device:TPU:1, one launch (start us, length us, event | category | flops | bytes accessed | tf_op | source)
XLA Modules:
  0.0 44.5 jit_solution(14191263701768558290)
XLA Ops:
  0.6 1.7 %pack.1 = (bf16[528,256]{1,0:T(8,128)(2,1)}, bf16[256,256]{1,0:T(8,128)(2,1)}) custom-call(s32[1,6]{1,0:T(1,128)} %blocks_ref.1, bf16[128,256]{1,0:T(8,128)(2,1)} %q_ref.1, bf16[128,256]{1,0:T(8,128)(2,1)} %k_ref.1, bf16[128,256]{1,0:T(8,128)(2,1)} %v_ref.1, bf16[128,256]{1,0:T(8,128)(2,1)} %g_ref.1), custom_call_target="tpu_custom_call" | custom-call | tf_op jit(solution)/shard_map/pack/pallas_call | solution.py:265
  2.3 8.9 %all-gather = bf16[1056,256]{1,0:T(8,128)(2,1)S(1)} all-gather(bf16[528,256]{1,0:T(8,128)(2,1)} %get-tuple-element.12), channel_id=2, replica_groups={{0,8},{16,24},{32,40},{48,56},{64,72},{80,88},{96,104},{112,120},{128,1..., dimensions={0}, use_global_device_ids=true | all-gather | bytes 811008 | tf_op jit(solution)/shard_map/all_gather | solution.py:260
  11.2 0.0 copy-start
  11.3 2.1 %collective-permute-start = (bf16[512,256]{1,0:T(8,128)(2,1)S(1)}, bf16[512,256]{1,0:T(8,128)(2,1)S(1)}, u32[]{:S(2)}, u32[]{:S(2)}) collective-permute-start(bf16[512,256]{1,0:T(8,128)(2,1)S(1)} %bitcast.8), channel_id=1, source_target_pairs={{0,16},{8,40},{16,32},{24,56},{32,48},{40,72},{48,64},{56,88},{64,... | collective-permute-start | bytes 786440 | tf_op jit(solution)/shard_map/ppermute | solution.py:257
  13.3 0.0 copy-done
  13.3 2.3 %collective-permute-start.1 = (bf16[256,256]{1,0:T(8,128)(2,1)S(1)}, bf16[256,256]{1,0:T(8,128)(2,1)S(1)}, u32[]{:S(2)}, u32[]{:S(2)}) collective-permute-start(bf16[256,256]{1,0:T(8,128)(2,1)S(1)} %copy-done), channel_id=1, source_target_pairs={{8,56},{24,72},{40,88},{56,104},{72,120},{88,136},{104,152},{120,1... | collective-permute-start | bytes 393224 | tf_op jit(solution)/shard_map/ppermute | solution.py:257
  15.6 7.9 %collective-permute-start.2 = (bf16[1056,128]{1,0:T(8,128)(2,1)S(1)}, bf16[1056,128]{1,0:T(8,128)(2,1)S(1)}, u32[]{:S(2)}, u32[]{:S(2)}) collective-permute-start(bf16[1056,128]{1,0:T(8,128)(2,1)S(1)} %slice_select_fusion.own_ref), channel_id=1, source_target_pairs={{0,496},{8,504},{16,0},{24,8},{32,16},{40,24},{48,32},{56,40},{64,... | collective-permute-start | bytes 811016 | tf_op jit(solution)/shard_map/ppermute | solution.py:257
  23.5 0.0 collective-permute-done.behind_ref
  23.6 5.8 %collective-permute-done.1.far_ref = bf16[256,256]{1,0:T(8,128)(2,1)S(1)} collective-permute-done((bf16[256,256]{1,0:T(8,128)(2,1)S(1)}, bf16[256,256]{1,0:T(8,128)(2,1)S(1)}, u32[]{:S(2)}, u32[]{:S(2)}) %collective-permute-start.1) | collective-permute-done | bytes 131104 | tf_op jit(solution)/shard_map/ppermute | solution.py:257
  29.4 2.1 %all-gather.1 = bf16[1536,128]{1,0:T(8,128)(2,1)S(1)} all-gather(bf16[768,128]{1,0:T(8,128)(2,1)S(1)} %slice_select_fusion.1), channel_id=3, replica_groups={{0,8},{16,24},{32,40},{48,56},{64,72},{80,88},{96,104},{112,120},{128,1..., dimensions={0}, use_global_device_ids=true | all-gather | bytes 589824 | tf_op jit(solution)/shard_map/all_gather | solution.py:260
  31.5 1.9 %own.1 = (bf16[896,128]{1,0:T(8,128)(2,1)S(1)}, bf16[896,128]{1,0:T(8,128)(2,1)S(1)}, bf16[256,128]{1,0:T(8,128)(2,1)S(1)}, f32[512,128]{1,0:T(8,128)S(1)}, f32[512,128]{1,0:T(8,128)S(1)}) custom-call(s32[1]{0:T(128)} %bitcast.core_ref, bf16[1056,128]{1,0:T(8,128)(2,1)S(1)} %slice_select_fusion.own_ref, ...), custom_call_target="tpu_custom_call" | custom-call | flops 201326592 | bytes 2000000 | tf_op jit(solution)/shard_map/own/pallas_call | solution.py:233
  33.5 0.0 collective-permute-done.2.ahead_ref
  33.5 0.9 %ahead.1 = (f32[512,128]{1,0:T(8,128)S(1)}, bf16[512,128]{1,0:T(8,128)(2,1)S(1)}) custom-call(bf16[1056,128]{1,0:T(8,128)(2,1)S(1)} %collective-permute-done.2.ahead_ref, bf16[896,128]{1,0:T(8,128)(2,1)S(1)} %get-tuple-element.15.keys7, bf16[896,128]{1,0:T(8,128)(2,1)S(1)} %get-tuple-element.16.values7, f32[512,128]{1,0:T(8,128)S(1)} %get-tuple-element.17.own_in, ...), custom_call_target="tpu_custom_call" | custom-call | flops 100663296 | bytes 1000000 | tf_op jit(solution)/shard_map/ahead/pallas_call | solution.py:233
  34.4 3.4 %collective-permute-start.3 = (bf16[512,128]{1,0:T(8,128)(2,1)S(1)}, bf16[512,128]{1,0:T(8,128)(2,1)S(1)}, u32[]{:S(2)}, u32[]{:S(2)}) collective-permute-start(bf16[512,128]{1,0:T(8,128)(2,1)S(1)} %get-tuple-element.20), channel_id=1, source_target_pairs={{0,480},{8,488},{16,496},{24,504},{32,0},{40,8},{48,16},{56,24},{6... | collective-permute-start | bytes 393224 | tf_op jit(solution)/shard_map/ppermute | solution.py:257
  37.8 0.8 %after.1.sums_ref = f32[512,128]{1,0:T(8,128)S(1)} custom-call(bf16[1056,128]{1,0:T(8,128)(2,1)S(1)} %collective-permute-done.2.ahead_ref, bf16[896,128]{1,0:T(8,128)(2,1)S(1)} %get-tuple-element.15.keys7, bf16[896,128]{1,0:T(8,128)(2,1)S(1)} %get-tuple-element.16.values7, f32[512,128]{1,0:T(8,128)S(1)} %get-tuple-element.19.own_in), custom_call_target="tpu_custom_call" | custom-call | flops 100663296 | bytes 1000000 | tf_op jit(solution)/shard_map/after/pallas_call | solution.py:233
  38.7 2.6 %collective-permute-done.3.back_ref = bf16[512,128]{1,0:T(8,128)(2,1)S(1)} collective-permute-done((bf16[512,128]{1,0:T(8,128)(2,1)S(1)}, bf16[512,128]{1,0:T(8,128)(2,1)S(1)}, u32[]{:S(2)}, u32[]{:S(2)}) %collective-permute-start.3) | collective-permute-done | bytes 131104 | tf_op jit(solution)/shard_map/ppermute | solution.py:257
  41.3 2.5 %all-gather.2 = bf16[768,128]{1,0:T(8,128)(2,1)S(1)} all-gather(bf16[384,128]{1,0:T(8,128)(2,1)S(1)} %swap.1), channel_id=4, replica_groups={{0,8},{16,24},{32,40},{48,56},{64,72},{80,88},{96,104},{112,120},{128,1..., dimensions={0}, use_global_device_ids=true | all-gather | bytes 294912 | tf_op jit(solution)/shard_map/all_gather | solution.py:260
  43.8 0.7 %last.1 = (bf16[128,256]{1,0:T(8,128)(2,1)}, bf16[128,256]{1,0:T(8,128)(2,1)}, bf16[128,256]{1,0:T(8,128)(2,1)}) custom-call(s32[1]{0:T(128)} %bitcast.core_ref, bf16[256,128]{1,0:T(8,128)(2,1)S(1)} %get-tuple-element.14.query_grad, f32[512,128]{1,0:T(8,128)S(1)} %after.1.sums_ref, bf16[512,128]{1,0:T(8,128)(2,1)S(1)} %collective-permute-done.3.back_ref, ...), custom_call_target="tpu_custom_call" | custom-call | tf_op jit(solution)/shard_map/last/pallas_call | solution.py:233
  (6 shorter events, 0.1 us)
Async XLA Ops:
  11.2 2.1 %copy-start = (bf16[256,256]{1,0:T(8,128)(2,1)S(1)}, bf16[256,256]{1,0:T(8,128)(2,1)}, u32[]{:S(2)}) copy-start(bf16[256,256]{1,0:T(8,128)(2,1)} %get-tuple-element.13) | copy-start | bytes 393220
  11.3 12.3 %collective-permute-start = (bf16[512,256]{1,0:T(8,128)(2,1)S(1)}, bf16[512,256]{1,0:T(8,128)(2,1)S(1)}, u32[]{:S(2)}, u32[]{:S(2)}) collective-permute-start(bf16[512,256]{1,0:T(8,128)(2,1)S(1)} %bitcast.8), channel_id=1, source_target_pairs={{0,16},{8,40},{16,32},{24,56},{32,48},{40,72},{48,64},{56,88},{64,... | collective-permute-start | bytes 786440 | tf_op jit(solution)/shard_map/ppermute | solution.py:257
  13.3 16.1 %collective-permute-start.1 = (bf16[256,256]{1,0:T(8,128)(2,1)S(1)}, bf16[256,256]{1,0:T(8,128)(2,1)S(1)}, u32[]{:S(2)}, u32[]{:S(2)}) collective-permute-start(bf16[256,256]{1,0:T(8,128)(2,1)S(1)} %copy-done), channel_id=1, source_target_pairs={{8,56},{24,72},{40,88},{56,104},{72,120},{88,136},{104,152},{120,1... | collective-permute-start | bytes 393224 | tf_op jit(solution)/shard_map/ppermute | solution.py:257
  15.6 17.8 %collective-permute-start.2 = (bf16[1056,128]{1,0:T(8,128)(2,1)S(1)}, bf16[1056,128]{1,0:T(8,128)(2,1)S(1)}, u32[]{:S(2)}, u32[]{:S(2)}) collective-permute-start(bf16[1056,128]{1,0:T(8,128)(2,1)S(1)} %slice_select_fusion.own_ref), channel_id=1, source_target_pairs={{0,496},{8,504},{16,0},{24,8},{32,16},{40,24},{48,32},{56,40},{64,... | collective-permute-start | bytes 811016 | tf_op jit(solution)/shard_map/ppermute | solution.py:257
  34.4 6.9 %collective-permute-start.3 = (bf16[512,128]{1,0:T(8,128)(2,1)S(1)}, bf16[512,128]{1,0:T(8,128)(2,1)S(1)}, u32[]{:S(2)}, u32[]{:S(2)}) collective-permute-start(bf16[512,128]{1,0:T(8,128)(2,1)S(1)} %get-tuple-element.20), channel_id=1, source_target_pairs={{0,480},{8,488},{16,496},{24,504},{32,0},{40,8},{48,16},{56,24},{6... | collective-permute-start | bytes 393224 | tf_op jit(solution)/shard_map/ppermute | solution.py:257

commit v3 on v2

--- a/solution.py
+++ b/solution.py
@@ -138,17 +138,14 @@
     }
 
 
-def own_kernel(
-    core_ref, own_ref, behind_ref, far_ref, got_ref,
-    keys, values, query_grad, own_sums, back_sums,
-):
+def own_kernel(core_ref, own_ref, behind_ref, far_ref, got_ref, keys, values, back_sums):
     every = slice(0, HALF)
 
     def place(mine, own):
         if mine == 0:
-            near, next_, last = (behind_ref, own, 0), (got_ref.at[1], every, 0), (got_ref.at[1], every, 4 * ROWS)
+            near, next_, last = (behind_ref, own, 0), (got_ref.at[1], every, 2 * ROWS), (got_ref.at[1], every, 0)
         else:
-            near, next_, last = (got_ref.at[0], every, 0), (behind_ref, own, 0), (far_ref, own, 0)
+            near, next_, last = (got_ref.at[0], every, 2 * ROWS), (behind_ref, own, 0), (far_ref, own, 0)
         for (ref, columns, start), first, count in ((last, 0, 1), (next_, 1, 2), (near, 3, 2)):
             for block in range(count):
                 take(ref, start + block * 2 * ROWS, 1, columns, keys, first + block)
@@ -162,42 +159,54 @@
         values[rows, :] = blocks[block][1]
     sums = {}
     for slot in range(2):
-        strip = slice(slot * ROWS, (slot + REACH) * ROWS)
-        strip_keys = keys[strip, :]
-        step = query_step(strip_keys, values[strip, :], *blocks[slot][2:], list(range(REACH)))
-        for p in range(REACH):
-            if slot + p not in (0, 3, 4):
-                dots(step, p, sums, slot + p)
-        query_grad[slot * ROWS : (slot + 1) * ROWS, :] = query_part(strip_keys, step[3])
-    write_sums(own_sums, sums, 5)
+        strip_step(slot, 0, blocks[slot], keys, values, [1 - slot, 2 - slot], sums)
     write_sums(back_sums, sums, 1)
 
 
-def ahead_step(slot, first, ahead_ref, keys, values, needed, sums):
+def strip_step(slot, first, block, keys, values, needed, sums):
     strip = slice((slot - first) * ROWS, (slot - first + REACH) * ROWS)
-    step = query_step(keys[strip, :], values[strip, :], *block_of(ahead_ref, slot - 2)[2:], needed)
+    step = query_step(keys[strip, :], values[strip, :], *block[2:], needed)
     for p in needed:
-        dots(step, p, sums, slot + p)
-
-
-def ahead_kernel(ahead_ref, keys7, values7, own_in, back_in, own_out, back_out, keys, values):
+        if slot + p in (1, 2, 5, 6):
+            dots(step, p, sums, slot + p)
+    return step
+
+
+def ahead_kernel(ahead_ref, keys7, values7, back_in, back_out, keys, values):
     for target, source, part in ((keys, keys7, 0), (values, values7, 1)):
         target[: 5 * ROWS, :] = source[2 * ROWS :, :]
         target[5 * ROWS :, :] = block_of(ahead_ref, 0)[part]
-    sums = read_sums(own_in, 5) | read_sums(back_in, 1)
-    ahead_step(2, 2, ahead_ref, keys, values, [0, 3, 4], sums)
-    write_sums(own_out, sums, 5)
+    sums = read_sums(back_in, 1)
+    strip_step(2, 2, block_of(ahead_ref, 0), keys, values, [0], sums)
     write_sums(back_out, sums, 1)
 
 
-def after_kernel(ahead_ref, keys7, values7, own_in, own_out, keys, values):
+def after_kernel(own_ref, ahead_ref, keys7, values7, query_grad, own_sums, keys, values):
     for target, source, part in ((keys, keys7, 0), (values, values7, 1)):
-        target[: 4 * ROWS, :] = source[3 * ROWS :, :]
+        target[: 7 * ROWS, :] = source[...]
         for block in range(2):
-            target[(4 + block) * ROWS : (5 + block) * ROWS, :] = block_of(ahead_ref, block)[part]
-    sums = read_sums(own_in, 5)
-    ahead_step(3, 3, ahead_ref, keys, values, [2, 3], sums)
-    write_sums(own_out, sums, 5)
+            target[(7 + block) * ROWS : (8 + block) * ROWS, :] = block_of(ahead_ref, block)[part]
+    sums = {}
+    for slot in range(4):
+        block = block_of((own_ref, ahead_ref)[slot // 2], slot % 2)
+        needed = list(range(REACH)) if slot < 2 else [5 - slot, 6 - slot]
+        if slot < 2:
+            strip = slice(slot * ROWS, (slot + REACH) * ROWS)
+            step = query_step(keys[strip, :], values[strip, :], *block[2:], needed)
+            for p in range(5 - slot, REACH):
+                dots(step, p, sums, slot + p)
+            query_grad[slot * ROWS : (slot + 1) * ROWS, :] = query_part(keys[strip, :], step[3])
+        else:
+            strip_step(slot, 0, block, keys, values, needed, sums)
+    write_sums(own_sums, sums, 5)
+
+
+def pick_kernel(core_ref, value_ref, out_ref):
+    def place(mine, own):
+        del own
+        out_ref[...] = value_ref[:, (1 - mine) * HALF : (2 - mine) * HALF]
+
+    on_core(core_ref[0], place)
 
 
 def total_of(sums_ref, back_ref, block, which):
@@ -277,20 +286,20 @@
     behind = send(pair[:, : 2 * ROWS].reshape(4 * ROWS, 2 * HALF), 1, 2)
     ours = half(pair.reshape(2 * MESSAGE, 2 * HALF), False)
     ahead = send(ours, -1, -1)
-    got = share(half(jnp.concatenate([behind, far], axis=0), True))
+    (far_half,) = call(pick_kernel, "pick", [((2 * ROWS, HALF), bf16)], (which, far), work=2)
+    got = share(jnp.concatenate([far_half, half(behind, True)], axis=0))
     seven, sums_of = ((7 * ROWS, HALF), bf16), (4 * ROWS, HALF)
-    keys7, values7, query_grad, sums, back = call(
-        own_kernel, "own", [seven, seven, ((2 * ROWS, HALF), bf16), (sums_of, f32), (sums_of, f32)],
-        (which, ours, behind, far, got), work=2,
-    )
-    sums, back = call(
-        ahead_kernel, "ahead", [(sums_of, f32), (sums_of, bf16)], (ahead, keys7, values7, sums, back),
+    keys7, values7, back = call(
+        own_kernel, "own", [seven, seven, (sums_of, f32)], (which, ours, behind, far, got), work=2
+    )
+    (back,) = call(
+        ahead_kernel, "ahead", [(sums_of, bf16)], (ahead, keys7, values7, back),
         (6 * ROWS, 6 * ROWS), work=1, scalar=False,
     )
     returned = send(back, -2, -2)
-    (sums,) = call(
-        after_kernel, "after", [(sums_of, f32)], (ahead, keys7, values7, sums), (6 * ROWS, 6 * ROWS),
-        work=1, scalar=False,
+    query_grad, sums = call(
+        after_kernel, "after", [((2 * ROWS, HALF), bf16), (sums_of, f32)], (ours, ahead, keys7, values7),
+        (9 * ROWS, 9 * ROWS), work=4, scalar=False,
     )
     (swap,) = call(
         swap_kernel, "swap", [((3 * ROWS, HALF), bf16)], (which, query_grad, sums, returned)

time: 44.8 us -> 42.8 us (0.955)
  waiting for transfers between devices: 8.45 us -> 0.16 us
  starting transfers between devices: 15.6 us -> 21.3 us
  Pallas kernels: 6.13 us -> 7.65 us
  blocking collectives: 13.5 us -> 12.6 us
    ppermute x4, waiting for transfers between devices: 8.45 us -> 0.16 us  [send(): return lax.ppermute(value, 'tm', pairs)]
    ppermute x4, starting transfers between devices: 15.6 us -> 21.3 us  [send(): return lax.ppermute(value, 'tm', pairs)]
    pallas_call x5 -> x6, Pallas kernels: 4.43 us -> 5.93 us  [call(): pl.pallas_call(kernel, name=name, out_shape=outs, in_specs=[SMEM] * scala...]
    all_gather x3, blocking collectives: 13.5 us -> 12.6 us  [share(): return lax.all_gather(value, 'tm', axis_index_groups=cores)]
  transfers between devices with their start and end apart: 4 -> 4, of which waited for: 2 -> 1; matrix products, arithmetic and copies ran while one was open for 0% -> 0% of each run, Pallas kernels for 6% -> 10%
where the time goes in v3:
time: 42.8 us; the launch traced here: 42.5 us
  starting transfers between devices  21.3 us (50%)
  blocking collectives  12.6 us (29%)
  Pallas kernels  7.65 us (18%)
  between operations  0.76 us (2%)
    ppermute x4, starting transfers between devices, send(): return lax.ppermute(value, 'tm', pairs)  21.3 us
    all_gather x3, blocking collectives, share(): return lax.all_gather(value, 'tm', axis_index_groups=cores)  12.6 us
    pallas_call x6, Pallas kernels, call(): pl.pallas_call(kernel, name=name, out_shape=outs, in_specs=[SMEM] * scala...  5.93 us
    pallas_call x1, Pallas kernels, on_device(): pl.pallas_call(pack_kernel, name='pack', out_shape=[jax.ShapeDtypeStruct(...  1.72 us
  transfers between devices with their start and end apart: 4, of which 1 were waited for; matrix products, arithmetic and copies ran while one was open for 0% of the time, Pallas kernels for 10%

profile of v3, /device:TPU:1, one launch (start us, length us, event | category | flops | bytes accessed | tf_op | source)
XLA Modules:
  0.0 42.5 jit_solution(9830715052888289982)
XLA Ops:
  0.6 1.7 %pack.1 = (bf16[528,256]{1,0:T(8,128)(2,1)}, bf16[256,256]{1,0:T(8,128)(2,1)}) custom-call(s32[1,6]{1,0:T(1,128)} %blocks_ref.1, bf16[128,256]{1,0:T(8,128)(2,1)} %q_ref.1, bf16[128,256]{1,0:T(8,128)(2,1)} %k_ref.1, bf16[128,256]{1,0:T(8,128)(2,1)} %v_ref.1, bf16[128,256]{1,0:T(8,128)(2,1)} %g_ref.1), custom_call_target="tpu_custom_call" | custom-call | tf_op jit(solution)/shard_map/pack/pallas_call | solution.py:274
  2.4 6.8 %collective-permute-start.2 = (bf16[256,256]{1,0:T(8,128)(2,1)}, bf16[256,256]{1,0:T(8,128)(2,1)S(1)}, u32[]{:S(2)}, u32[]{:S(2)}) collective-permute-start(bf16[256,256]{1,0:T(8,128)(2,1)} %get-tuple-element.11), channel_id=1, source_target_pairs={{8,56},{24,72},{40,88},{56,104},{72,120},{88,136},{104,152},{120,1... | collective-permute-start | bytes 393224 | tf_op jit(solution)/shard_map/ppermute | solution.py:266
  9.2 2.7 %all-gather = bf16[1056,256]{1,0:T(8,128)(2,1)S(1)} all-gather(bf16[528,256]{1,0:T(8,128)(2,1)} %get-tuple-element.10), channel_id=2, replica_groups={{0,8},{16,24},{32,40},{48,56},{64,72},{80,88},{96,104},{112,120},{128,1..., dimensions={0}, use_global_device_ids=true | all-gather | bytes 811008 | tf_op jit(solution)/shard_map/all_gather | solution.py:269
  11.9 3.2 %collective-permute-start.1 = (bf16[512,256]{1,0:T(8,128)(2,1)S(1)}, bf16[512,256]{1,0:T(8,128)(2,1)S(1)}, u32[]{:S(2)}, u32[]{:S(2)}) collective-permute-start(bf16[512,256]{1,0:T(8,128)(2,1)S(1)} %bitcast.8), channel_id=1, source_target_pairs={{0,16},{8,40},{16,32},{24,56},{32,48},{40,72},{48,64},{56,88},{64,... | collective-permute-start | bytes 786440 | tf_op jit(solution)/shard_map/ppermute | solution.py:266
  15.2 7.9 %collective-permute-start = (bf16[1056,128]{1,0:T(8,128)(2,1)S(1)}, bf16[1056,128]{1,0:T(8,128)(2,1)S(1)}, u32[]{:S(2)}, u32[]{:S(2)}) collective-permute-start(bf16[1056,128]{1,0:T(8,128)(2,1)S(1)} %slice_select_fusion.own_ref), channel_id=1, source_target_pairs={{0,496},{8,504},{16,0},{24,8},{32,16},{40,24},{48,32},{56,40},{64,... | collective-permute-start | bytes 811016 | tf_op jit(solution)/shard_map/ppermute | solution.py:266
  23.1 0.0 collective-permute-done.2.value_ref.far_ref
  23.1 0.0 collective-permute-done.1.behind_ref
  23.2 7.0 %all-gather.1 = bf16[1536,128]{1,0:T(8,128)(2,1)S(1)} all-gather(bf16[768,128]{1,0:T(8,128)(2,1)S(1)} %pad_maximum_fusion), channel_id=3, replica_groups={{0,8},{16,24},{32,40},{48,56},{64,72},{80,88},{96,104},{112,120},{128,1..., dimensions={0}, use_global_device_ids=true | all-gather | bytes 589824 | tf_op jit(solution)/shard_map/all_gather | solution.py:269
  30.2 1.3 %own.1 = (bf16[896,128]{1,0:T(8,128)(2,1)S(1)}, bf16[896,128]{1,0:T(8,128)(2,1)S(1)}, f32[512,128]{1,0:T(8,128)S(1)}) custom-call(s32[1]{0:T(128)} %bitcast.core_ref, bf16[1056,128]{1,0:T(8,128)(2,1)S(1)} %slice_select_fusion.own_ref, bf16[512,256]{1,0:T(8,128)(2,1)S(1)} %collective-permute-done.1.behind_ref, ...), custom_call_target="tpu_custom_call" | custom-call | flops 201326592 | bytes 2000000 | tf_op jit(solution)/shard_map/own/pallas_call | solution.py:242
  31.6 0.0 collective-permute-done.ahead_ref
  31.6 0.8 %ahead.1 = bf16[512,128]{1,0:T(8,128)(2,1)S(1)} custom-call(bf16[1056,128]{1,0:T(8,128)(2,1)S(1)} %collective-permute-done.ahead_ref, bf16[896,128]{1,0:T(8,128)(2,1)S(1)} %get-tuple-element.12.keys7, bf16[896,128]{1,0:T(8,128)(2,1)S(1)} %get-tuple-element.13.values7, f32[512,128]{1,0:T(8,128)S(1)} %get-tuple-element.16.back_in), custom_call_target="tpu_custom_call" | custom-call | flops 100663296 | bytes 1000000 | tf_op jit(solution)/shard_map/ahead/pallas_call | solution.py:242
  32.4 3.4 %collective-permute-start.3 = (bf16[512,128]{1,0:T(8,128)(2,1)S(1)}, bf16[512,128]{1,0:T(8,128)(2,1)S(1)}, u32[]{:S(2)}, u32[]{:S(2)}) collective-permute-start(bf16[512,128]{1,0:T(8,128)(2,1)S(1)} %ahead.1), channel_id=1, source_target_pairs={{0,480},{8,488},{16,496},{24,504},{32,0},{40,8},{48,16},{56,24},{6... | collective-permute-start | bytes 393224 | tf_op jit(solution)/shard_map/ppermute | solution.py:266
  35.7 3.1 %after.1 = (bf16[256,128]{1,0:T(8,128)(2,1)S(1)}, f32[512,128]{1,0:T(8,128)S(1)}) custom-call(bf16[1056,128]{1,0:T(8,128)(2,1)S(1)} %slice_select_fusion.own_ref, bf16[1056,128]{1,0:T(8,128)(2,1)S(1)} %collective-permute-done.ahead_ref, bf16[896,128]{1,0:T(8,128)(2,1)S(1)} %get-tuple-element.12.keys7, bf16[896,128]{1,0:T(8,128)(2,1)S(1)} %get-tuple-element.13.values7), custom_call_target="tpu_custom_call" | custom-call | flops 402653184 | bytes 4000000 | tf_op jit(solution)/shard_map/after/pallas_call | solution.py:242
  38.8 0.2 collective-permute-done.3.back_ref
  39.0 2.8 %all-gather.2 = bf16[768,128]{1,0:T(8,128)(2,1)S(1)} all-gather(bf16[384,128]{1,0:T(8,128)(2,1)S(1)} %swap.1), channel_id=4, replica_groups={{0,8},{16,24},{32,40},{48,56},{64,72},{80,88},{96,104},{112,120},{128,1..., dimensions={0}, use_global_device_ids=true | all-gather | bytes 294912 | tf_op jit(solution)/shard_map/all_gather | solution.py:269
  41.8 0.7 %last.1 = (bf16[128,256]{1,0:T(8,128)(2,1)}, bf16[128,256]{1,0:T(8,128)(2,1)}, bf16[128,256]{1,0:T(8,128)(2,1)}) custom-call(s32[1]{0:T(128)} %bitcast.core_ref, bf16[256,128]{1,0:T(8,128)(2,1)S(1)} %get-tuple-element.14.query_grad, f32[512,128]{1,0:T(8,128)S(1)} %get-tuple-element.15.sums_ref, bf16[512,128]{1,0:T(8,128)(2,1)S(1)} %collective-permute-done.3.back_ref, ...), custom_call_target="tpu_custom_call" | custom-call | tf_op jit(solution)/shard_map/last/pallas_call | solution.py:242
  (6 shorter events, 0.1 us)
Async XLA Ops:
  2.4 20.8 %collective-permute-start.2 = (bf16[256,256]{1,0:T(8,128)(2,1)}, bf16[256,256]{1,0:T(8,128)(2,1)S(1)}, u32[]{:S(2)}, u32[]{:S(2)}) collective-permute-start(bf16[256,256]{1,0:T(8,128)(2,1)} %get-tuple-element.11), channel_id=1, source_target_pairs={{8,56},{24,72},{40,88},{56,104},{72,120},{88,136},{104,152},{120,1... | collective-permute-start | bytes 393224 | tf_op jit(solution)/shard_map/ppermute | solution.py:266
  11.9 11.2 %collective-permute-start.1 = (bf16[512,256]{1,0:T(8,128)(2,1)S(1)}, bf16[512,256]{1,0:T(8,128)(2,1)S(1)}, u32[]{:S(2)}, u32[]{:S(2)}) collective-permute-start(bf16[512,256]{1,0:T(8,128)(2,1)S(1)} %bitcast.8), channel_id=1, source_target_pairs={{0,16},{8,40},{16,32},{24,56},{32,48},{40,72},{48,64},{56,88},{64,... | collective-permute-start | bytes 786440 | tf_op jit(solution)/shard_map/ppermute | solution.py:266
  15.2 16.3 %collective-permute-start = (bf16[1056,128]{1,0:T(8,128)(2,1)S(1)}, bf16[1056,128]{1,0:T(8,128)(2,1)S(1)}, u32[]{:S(2)}, u32[]{:S(2)}) collective-permute-start(bf16[1056,128]{1,0:T(8,128)(2,1)S(1)} %slice_select_fusion.own_ref), channel_id=1, source_target_pairs={{0,496},{8,504},{16,0},{24,8},{32,16},{40,24},{48,32},{56,40},{64,... | collective-permute-start | bytes 811016 | tf_op jit(solution)/shard_map/ppermute | solution.py:266
  32.4 6.6 %collective-permute-start.3 = (bf16[512,128]{1,0:T(8,128)(2,1)S(1)}, bf16[512,128]{1,0:T(8,128)(2,1)S(1)}, u32[]{:S(2)}, u32[]{:S(2)}) collective-permute-start(bf16[512,128]{1,0:T(8,128)(2,1)S(1)} %ahead.1), channel_id=1, source_target_pairs={{0,480},{8,488},{16,496},{24,504},{32,0},{40,8},{48,16},{56,24},{6... | collective-permute-start | bytes 393224 | tf_op jit(solution)/shard_map/ppermute | solution.py:266

commit v4 on v3

--- a/solution.py
+++ b/solution.py
@@ -20,19 +20,13 @@
 SMEM = pl.BlockSpec(memory_space=pltpu.SMEM)
 
 
-def pack_kernel(blocks_ref, q_ref, k_ref, v_ref, g_ref, out_ref, pair_ref):
-    for ref, start in ((k_ref, 0), (v_ref, ROWS)):
-        rows = ref[...]
-        out_ref[start : start + ROWS, :] = rows
-        pair_ref[start : start + ROWS, :] = rows
-    out_ref[2 * ROWS : 3 * ROWS, :] = q_ref[...]
-    out_ref[3 * ROWS : 4 * ROWS, :] = g_ref[...]
-    row = lax.broadcasted_iota(jnp.int32, (FLAGS, 2 * HALF), 0)
-    flags = jnp.zeros((FLAGS, 2 * HALF), jnp.float32)
-    for distance in range(REACH):
-        live = (blocks_ref[0, distance] >= 0).astype(jnp.float32)
-        flags = jnp.where(row == distance, live, flags)
-    out_ref[4 * ROWS :, :] = flags.astype(jnp.bfloat16)
+def placed(parts, rows, columns):
+    total = None
+    for part, row, column in parts:
+        space = [(row, rows - row - part.shape[0], 0), (column, columns - column - part.shape[1], 0)]
+        padded = lax.pad(part, jnp.array(-jnp.inf, part.dtype), space)
+        total = padded if total is None else jnp.maximum(total, padded)
+    return total
 
 
 def by_head(rows):
@@ -54,6 +48,10 @@
         @pl.when(core == mine)
         def _(mine=mine):
             place(mine, own[mine])
+
+
+def live_at(live, distance):
+    return jnp.broadcast_to(live[:1, distance : distance + 1], (1, 2 * ROWS)) > 0.0
 
 
 def query_step(strip_keys, strip_values, query_rows, grad_rows, live, needed):
@@ -65,14 +63,13 @@
     query_heads = by_head(query_rows)
     grad_heads = by_head(grad_rows)
     live = live.astype(jnp.float32)
-    live = jnp.concatenate([live, live], axis=1)
     scores = lax.dot_general(strip_keys, query_heads, both, preferred_element_type=jnp.float32)
     prob_grad = lax.dot_general(
         strip_values, grad_heads, both, preferred_element_type=jnp.float32
     )
     pieces = [scores[p * ROWS : (p + 1) * ROWS] for p in range(REACH)]
-    pieces[0] = jnp.where(live[5:6, :] > 0.0, pieces[0], MASKED)
-    pieces[1] = jnp.where(live[4:5, :] > 0.0, pieces[1], MASKED)
+    pieces[0] = jnp.where(live_at(live, 5), pieces[0], MASKED)
+    pieces[1] = jnp.where(live_at(live, 4), pieces[1], MASKED)
     pieces[5] = jnp.where(key_row <= query_row, pieces[5], MASKED)
     grad_pieces = [prob_grad[p * ROWS : (p + 1) * ROWS] for p in range(REACH)]
     peak = pieces[0]
@@ -271,17 +268,11 @@
     def half(value, other):
         return jnp.where((core == 0) != other, value[:, :HALF], value[:, HALF:])
 
-    own, own_pair = pl.pallas_call(
-        pack_kernel,
-        name="pack",
-        out_shape=[
-            jax.ShapeDtypeStruct((MESSAGE, 2 * HALF), bf16),
-            jax.ShapeDtypeStruct((2 * ROWS, 2 * HALF), bf16),
-        ],
-        in_specs=[SMEM] + [VMEM] * 4,
-        out_specs=[VMEM] * 2,
-    )(key_blocks, queries, keys, values, out_grad)
-    far = send(own_pair, 0, 3)
+    live = (key_blocks >= 0).astype(bf16)
+    parts = [(x, i * ROWS, 0) for i, x in enumerate((keys, values, queries, out_grad))]
+    parts += [(live, 4 * ROWS, 0), (live, 4 * ROWS, HALF)]
+    own = placed(parts, MESSAGE, 2 * HALF)
+    far = send(own[: 2 * ROWS], 0, 3)
     pair = share(own)
     behind = send(pair[:, : 2 * ROWS].reshape(4 * ROWS, 2 * HALF), 1, 2)
     ours = half(pair.reshape(2 * MESSAGE, 2 * HALF), False)

time: 42.8 us -> 42.5 us (level)
  other arithmetic: 0.07 us -> 1.69 us
  Pallas kernels: 7.65 us -> 6.04 us
    pallas_call x1 -> x0, Pallas kernels: 1.72 us -> none  [on_device(): pl.pallas_call(pack_kernel, name='pack', out_shape=[jax.ShapeDtypeStruct(...]
    max x0 -> x1, other arithmetic: none -> 0.95 us  [placed(): total = padded if total is None else jnp.maximum(total, padded)]
    convert_element_type x0 -> x1, other arithmetic: none -> 0.66 us  [on_device(): live = (key_blocks >= 0).astype(bf16)]
  transfers between devices with their start and end apart: 4 -> 4, of which waited for: 1 -> 0; matrix products, arithmetic and copies ran while one was open for 0% -> 0% of each run, Pallas kernels for 10% -> 11%
where the time goes in v4:
time: 42.5 us; the launch traced here: 42.2 us
  starting transfers between devices  21.3 us (50%)
  blocking collectives  12.3 us (29%)
  Pallas kernels  6.04 us (14%)
  other arithmetic  1.69 us (4%)
  between operations  0.77 us (2%)
    ppermute x4, starting transfers between devices, send(): return lax.ppermute(value, 'tm', pairs)  21.3 us
    all_gather x3, blocking collectives, share(): return lax.all_gather(value, 'tm', axis_index_groups=cores)  12.3 us
    pallas_call x6, Pallas kernels, call(): pl.pallas_call(kernel, name=name, out_shape=outs, in_specs=[SMEM] * scala...  6.04 us
    max x1, other arithmetic, placed(): total = padded if total is None else jnp.maximum(total, padded)  0.95 us
  transfers between devices with their start and end apart: 4, of which 0 were waited for; matrix products, arithmetic and copies ran while one was open for 0% of the time, Pallas kernels for 11%

profile of v4, /device:TPU:1, one launch (start us, length us, event | category | flops | bytes accessed | tf_op | source)
XLA Modules:
  0.0 42.2 jit_solution(4643946023139312888)
XLA Ops:
  0.6 0.7 %compare_convert_fusion = bf16[1,6]{1,0:T(2,128)(2,1)S(1)} fusion(s32[1,6]{1,0:T(1,128)} %param.9), kind=kLoop, calls=%fused_computation.4 | loop fusion | flops 12 | bytes 36 | tf_op jit(solution)/shard_map/convert_element_type | solution.py:271
  1.3 1.0 %pad_maximum_fusion = bf16[528,256]{1,0:T(8,128)(2,1)S(1)} fusion(bf16[1,6]{1,0:T(2,128)(2,1)S(1)} %compare_convert_fusion, bf16[128,256]{1,0:T(8,128)(2,1)} %param.8, bf16[128,256]{1,0:T(8,128)(2,1)} %param.5, bf16[128,256]{1,0:T(8,128)(2,1)} %param.7, bf16[128,256]{1,0:T(8,128)(2,1)} %param.6), kind=kLoop, calls=%fused_computation.1 | loop fusion | flops 1622016 | bytes 532492 | tf_op jit(solution)/shard_map/max | solution.py:28
  2.3 6.8 %collective-permute-start.2 = (bf16[256,256]{1,0:T(8,128)(2,1)S(1)}, bf16[256,256]{1,0:T(8,128)(2,1)S(1)}, u32[]{:S(2)}, u32[]{:S(2)}) collective-permute-start(bf16[256,256]{1,0:T(8,128)(2,1)S(1)} %slice.27), channel_id=1, source_target_pairs={{8,56},{24,72},{40,88},{56,104},{72,120},{88,136},{104,152},{120,1... | collective-permute-start | bytes 393224 | tf_op jit(solution)/shard_map/ppermute | solution.py:263
  9.1 2.5 %all-gather = bf16[1056,256]{1,0:T(8,128)(2,1)S(1)} all-gather(bf16[528,256]{1,0:T(8,128)(2,1)S(1)} %pad_maximum_fusion), channel_id=2, replica_groups={{0,8},{16,24},{32,40},{48,56},{64,72},{80,88},{96,104},{112,120},{128,1..., dimensions={0}, use_global_device_ids=true | all-gather | bytes 811008 | tf_op jit(solution)/shard_map/all_gather | solution.py:266
  11.7 3.2 %collective-permute-start.1 = (bf16[512,256]{1,0:T(8,128)(2,1)S(1)}, bf16[512,256]{1,0:T(8,128)(2,1)S(1)}, u32[]{:S(2)}, u32[]{:S(2)}) collective-permute-start(bf16[512,256]{1,0:T(8,128)(2,1)S(1)} %bitcast.8), channel_id=1, source_target_pairs={{0,16},{8,40},{16,32},{24,56},{32,48},{40,72},{48,64},{56,88},{64,... | collective-permute-start | bytes 786440 | tf_op jit(solution)/shard_map/ppermute | solution.py:263
  14.9 7.9 %collective-permute-start = (bf16[1056,128]{1,0:T(8,128)(2,1)S(1)}, bf16[1056,128]{1,0:T(8,128)(2,1)S(1)}, u32[]{:S(2)}, u32[]{:S(2)}) collective-permute-start(bf16[1056,128]{1,0:T(8,128)(2,1)S(1)} %slice_select_fusion.own_ref), channel_id=1, source_target_pairs={{0,496},{8,504},{16,0},{24,8},{32,16},{40,24},{48,32},{56,40},{64,... | collective-permute-start | bytes 811016 | tf_op jit(solution)/shard_map/ppermute | solution.py:263
  22.8 0.0 collective-permute-done.2.value_ref.far_ref
  22.9 0.0 collective-permute-done.1.behind_ref
  22.9 7.0 %all-gather.1 = bf16[1536,128]{1,0:T(8,128)(2,1)S(1)} all-gather(bf16[768,128]{1,0:T(8,128)(2,1)S(1)} %pad_maximum_fusion.1), channel_id=3, replica_groups={{0,8},{16,24},{32,40},{48,56},{64,72},{80,88},{96,104},{112,120},{128,1..., dimensions={0}, use_global_device_ids=true | all-gather | bytes 589824 | tf_op jit(solution)/shard_map/all_gather | solution.py:266
  29.9 1.3 %own.1 = (bf16[896,128]{1,0:T(8,128)(2,1)S(1)}, bf16[896,128]{1,0:T(8,128)(2,1)S(1)}, f32[512,128]{1,0:T(8,128)S(1)}) custom-call(s32[1]{0:T(128)} %bitcast.core_ref, bf16[1056,128]{1,0:T(8,128)(2,1)S(1)} %slice_select_fusion.own_ref, bf16[512,256]{1,0:T(8,128)(2,1)S(1)} %collective-permute-done.1.behind_ref, ...), custom_call_target="tpu_custom_call" | custom-call | flops 201326592 | bytes 2000000 | tf_op jit(solution)/shard_map/own/pallas_call | solution.py:239
  31.3 0.0 collective-permute-done.ahead_ref
  31.3 0.8 %ahead.1 = bf16[512,128]{1,0:T(8,128)(2,1)S(1)} custom-call(bf16[1056,128]{1,0:T(8,128)(2,1)S(1)} %collective-permute-done.ahead_ref, bf16[896,128]{1,0:T(8,128)(2,1)S(1)} %get-tuple-element.8.keys7, bf16[896,128]{1,0:T(8,128)(2,1)S(1)} %get-tuple-element.9.values7, f32[512,128]{1,0:T(8,128)S(1)} %get-tuple-element.12.back_in), custom_call_target="tpu_custom_call" | custom-call | flops 100663296 | bytes 1000000 | tf_op jit(solution)/shard_map/ahead/pallas_call | solution.py:239
  32.1 3.4 %collective-permute-start.3 = (bf16[512,128]{1,0:T(8,128)(2,1)S(1)}, bf16[512,128]{1,0:T(8,128)(2,1)S(1)}, u32[]{:S(2)}, u32[]{:S(2)}) collective-permute-start(bf16[512,128]{1,0:T(8,128)(2,1)S(1)} %ahead.1), channel_id=1, source_target_pairs={{0,480},{8,488},{16,496},{24,504},{32,0},{40,8},{48,16},{56,24},{6... | collective-permute-start | bytes 393224 | tf_op jit(solution)/shard_map/ppermute | solution.py:263
  35.4 3.2 %after.1 = (bf16[256,128]{1,0:T(8,128)(2,1)S(1)}, f32[512,128]{1,0:T(8,128)S(1)}) custom-call(bf16[1056,128]{1,0:T(8,128)(2,1)S(1)} %slice_select_fusion.own_ref, bf16[1056,128]{1,0:T(8,128)(2,1)S(1)} %collective-permute-done.ahead_ref, bf16[896,128]{1,0:T(8,128)(2,1)S(1)} %get-tuple-element.8.keys7, bf16[896,128]{1,0:T(8,128)(2,1)S(1)} %get-tuple-element.9.values7), custom_call_target="tpu_custom_call" | custom-call | flops 402653184 | bytes 4000000 | tf_op jit(solution)/shard_map/after/pallas_call | solution.py:239
  38.6 0.0 collective-permute-done.3.back_ref
  38.7 2.8 %all-gather.2 = bf16[768,128]{1,0:T(8,128)(2,1)S(1)} all-gather(bf16[384,128]{1,0:T(8,128)(2,1)S(1)} %swap.1), channel_id=4, replica_groups={{0,8},{16,24},{32,40},{48,56},{64,72},{80,88},{96,104},{112,120},{128,1..., dimensions={0}, use_global_device_ids=true | all-gather | bytes 294912 | tf_op jit(solution)/shard_map/all_gather | solution.py:266
  41.5 0.7 %last.1 = (bf16[128,256]{1,0:T(8,128)(2,1)}, bf16[128,256]{1,0:T(8,128)(2,1)}, bf16[128,256]{1,0:T(8,128)(2,1)}) custom-call(s32[1]{0:T(128)} %bitcast.core_ref, bf16[256,128]{1,0:T(8,128)(2,1)S(1)} %get-tuple-element.10.query_grad, f32[512,128]{1,0:T(8,128)S(1)} %get-tuple-element.11.sums_ref, bf16[512,128]{1,0:T(8,128)(2,1)S(1)} %collective-permute-done.3.back_ref, ...), custom_call_target="tpu_custom_call" | custom-call | tf_op jit(solution)/shard_map/last/pallas_call | solution.py:239
  (7 shorter events, 0.1 us)
Async XLA Ops:
  2.3 20.6 %collective-permute-start.2 = (bf16[256,256]{1,0:T(8,128)(2,1)S(1)}, bf16[256,256]{1,0:T(8,128)(2,1)S(1)}, u32[]{:S(2)}, u32[]{:S(2)}) collective-permute-start(bf16[256,256]{1,0:T(8,128)(2,1)S(1)} %slice.27), channel_id=1, source_target_pairs={{8,56},{24,72},{40,88},{56,104},{72,120},{88,136},{104,152},{120,1... | collective-permute-start | bytes 393224 | tf_op jit(solution)/shard_map/ppermute | solution.py:263
  11.7 11.2 %collective-permute-start.1 = (bf16[512,256]{1,0:T(8,128)(2,1)S(1)}, bf16[512,256]{1,0:T(8,128)(2,1)S(1)}, u32[]{:S(2)}, u32[]{:S(2)}) collective-permute-start(bf16[512,256]{1,0:T(8,128)(2,1)S(1)} %bitcast.8), channel_id=1, source_target_pairs={{0,16},{8,40},{16,32},{24,56},{32,48},{40,72},{48,64},{56,88},{64,... | collective-permute-start | bytes 786440 | tf_op jit(solution)/shard_map/ppermute | solution.py:263
  14.9 16.3 %collective-permute-start = (bf16[1056,128]{1,0:T(8,128)(2,1)S(1)}, bf16[1056,128]{1,0:T(8,128)(2,1)S(1)}, u32[]{:S(2)}, u32[]{:S(2)}) collective-permute-start(bf16[1056,128]{1,0:T(8,128)(2,1)S(1)} %slice_select_fusion.own_ref), channel_id=1, source_target_pairs={{0,496},{8,504},{16,0},{24,8},{32,16},{40,24},{48,32},{56,40},{64,... | collective-permute-start | bytes 811016 | tf_op jit(solution)/shard_map/ppermute | solution.py:263
  32.1 6.6 %collective-permute-start.3 = (bf16[512,128]{1,0:T(8,128)(2,1)S(1)}, bf16[512,128]{1,0:T(8,128)(2,1)S(1)}, u32[]{:S(2)}, u32[]{:S(2)}) collective-permute-start(bf16[512,128]{1,0:T(8,128)(2,1)S(1)} %ahead.1), channel_id=1, source_target_pairs={{0,480},{8,488},{16,496},{24,504},{32,0},{40,8},{48,16},{56,24},{6... | collective-permute-start | bytes 393224 | tf_op jit(solution)/shard_map/ppermute | solution.py:263

commit v5 on v4

--- a/solution.py
+++ b/solution.py
@@ -140,9 +140,9 @@
 
     def place(mine, own):
         if mine == 0:
-            near, next_, last = (behind_ref, own, 0), (got_ref.at[1], every, 2 * ROWS), (got_ref.at[1], every, 0)
+            near, next_, last = (got_ref.at[1], every, 2 * ROWS), (behind_ref, own, 0), (got_ref.at[1], every, 0)
         else:
-            near, next_, last = (got_ref.at[0], every, 2 * ROWS), (behind_ref, own, 0), (far_ref, own, 0)
+            near, next_, last = (behind_ref, own, 0), (got_ref.at[0], every, 2 * ROWS), (far_ref, own, 0)
         for (ref, columns, start), first, count in ((last, 0, 1), (next_, 1, 2), (near, 3, 2)):
             for block in range(count):
                 take(ref, start + block * 2 * ROWS, 1, columns, keys, first + block)
@@ -274,7 +274,7 @@
     own = placed(parts, MESSAGE, 2 * HALF)
     far = send(own[: 2 * ROWS], 0, 3)
     pair = share(own)
-    behind = send(pair[:, : 2 * ROWS].reshape(4 * ROWS, 2 * HALF), 1, 2)
+    behind = send(pair[:, : 2 * ROWS].reshape(4 * ROWS, 2 * HALF), 2, 1)
     ours = half(pair.reshape(2 * MESSAGE, 2 * HALF), False)
     ahead = send(ours, -1, -1)
     (far_half,) = call(pick_kernel, "pick", [((2 * ROWS, HALF), bf16)], (which, far), work=2)

time: 42.5 us -> 41.7 us (0.981)
  blocking collectives: 12.3 us -> 7.07 us
  waiting for transfers between devices: 0.05 us -> 4.31 us
    all_gather x3, blocking collectives: 12.3 us -> 7.07 us  [share(): return lax.all_gather(value, 'tm', axis_index_groups=cores)]
    ppermute x4, waiting for transfers between devices: 0.05 us -> 4.31 us  [send(): return lax.ppermute(value, 'tm', pairs)]
  transfers between devices with their start and end apart: 4 -> 4, of which waited for: 0 -> 2; matrix products, arithmetic and copies ran while one was open for 0% -> 0% of each run, Pallas kernels for 11% -> 11%
where the time goes in v5:
time: 41.7 us; the launch traced here: 41.5 us
  starting transfers between devices  21.6 us (52%)
  blocking collectives  7.07 us (17%)
  Pallas kernels  6.04 us (14%)
  waiting for transfers between devices  4.31 us (10%)
  other arithmetic  1.68 us (4%)
  between operations  0.75 us (2%)
    ppermute x4, starting transfers between devices, send(): return lax.ppermute(value, 'tm', pairs)  21.6 us
    all_gather x3, blocking collectives, share(): return lax.all_gather(value, 'tm', axis_index_groups=cores)  7.07 us
    pallas_call x6, Pallas kernels, call(): pl.pallas_call(kernel, name=name, out_shape=outs, in_specs=[SMEM] * scala...  6.04 us
    ppermute x4, waiting for transfers between devices, send(): return lax.ppermute(value, 'tm', pairs)  4.31 us
    max x1, other arithmetic, placed(): total = padded if total is None else jnp.maximum(total, padded)  0.95 us
  transfers between devices with their start and end apart: 4, of which 2 were waited for; matrix products, arithmetic and copies ran while one was open for 0% of the time, Pallas kernels for 11%

profile of v5, /device:TPU:1, one launch (start us, length us, event | category | flops | bytes accessed | tf_op | source)
XLA Modules:
  0.0 41.5 jit_solution(2317054088484036813)
XLA Ops:
  0.6 0.7 %compare_convert_fusion = bf16[1,6]{1,0:T(2,128)(2,1)S(1)} fusion(s32[1,6]{1,0:T(1,128)} %param.9), kind=kLoop, calls=%fused_computation.4 | loop fusion | flops 12 | bytes 36 | tf_op jit(solution)/shard_map/convert_element_type | solution.py:271
  1.3 1.0 %pad_maximum_fusion = bf16[528,256]{1,0:T(8,128)(2,1)S(1)} fusion(bf16[1,6]{1,0:T(2,128)(2,1)S(1)} %compare_convert_fusion, bf16[128,256]{1,0:T(8,128)(2,1)} %param.8, bf16[128,256]{1,0:T(8,128)(2,1)} %param.5, bf16[128,256]{1,0:T(8,128)(2,1)} %param.7, bf16[128,256]{1,0:T(8,128)(2,1)} %param.6), kind=kLoop, calls=%fused_computation.1 | loop fusion | flops 1622016 | bytes 532492 | tf_op jit(solution)/shard_map/max | solution.py:28
  2.3 6.8 %collective-permute-start.2 = (bf16[256,256]{1,0:T(8,128)(2,1)S(1)}, bf16[256,256]{1,0:T(8,128)(2,1)S(1)}, u32[]{:S(2)}, u32[]{:S(2)}) collective-permute-start(bf16[256,256]{1,0:T(8,128)(2,1)S(1)} %slice.27), channel_id=1, source_target_pairs={{8,56},{24,72},{40,88},{56,104},{72,120},{88,136},{104,152},{120,1... | collective-permute-start | bytes 393224 | tf_op jit(solution)/shard_map/ppermute | solution.py:263
  9.1 2.5 %all-gather = bf16[1056,256]{1,0:T(8,128)(2,1)S(1)} all-gather(bf16[528,256]{1,0:T(8,128)(2,1)S(1)} %pad_maximum_fusion), channel_id=2, replica_groups={{0,8},{16,24},{32,40},{48,56},{64,72},{80,88},{96,104},{112,120},{128,1..., dimensions={0}, use_global_device_ids=true | all-gather | bytes 811008 | tf_op jit(solution)/shard_map/all_gather | solution.py:266
  11.7 3.2 %collective-permute-start.1 = (bf16[512,256]{1,0:T(8,128)(2,1)S(1)}, bf16[512,256]{1,0:T(8,128)(2,1)S(1)}, u32[]{:S(2)}, u32[]{:S(2)}) collective-permute-start(bf16[512,256]{1,0:T(8,128)(2,1)S(1)} %bitcast.8), channel_id=1, source_target_pairs={{0,32},{8,24},{16,48},{24,40},{32,64},{40,56},{48,80},{56,72},{64,... | collective-permute-start | bytes 786440 | tf_op jit(solution)/shard_map/ppermute | solution.py:263
  14.9 7.9 %collective-permute-start = (bf16[1056,128]{1,0:T(8,128)(2,1)S(1)}, bf16[1056,128]{1,0:T(8,128)(2,1)S(1)}, u32[]{:S(2)}, u32[]{:S(2)}) collective-permute-start(bf16[1056,128]{1,0:T(8,128)(2,1)S(1)} %slice_select_fusion.own_ref), channel_id=1, source_target_pairs={{0,496},{8,504},{16,0},{24,8},{32,16},{40,24},{48,32},{56,40},{64,... | collective-permute-start | bytes 811016 | tf_op jit(solution)/shard_map/ppermute | solution.py:263
  22.8 0.0 collective-permute-done.2.value_ref.far_ref
  22.9 4.2 %collective-permute-done.1.behind_ref = bf16[512,256]{1,0:T(8,128)(2,1)S(1)} collective-permute-done((bf16[512,256]{1,0:T(8,128)(2,1)S(1)}, bf16[512,256]{1,0:T(8,128)(2,1)S(1)}, u32[]{:S(2)}, u32[]{:S(2)}) %collective-permute-start.1) | collective-permute-done | bytes 262176 | tf_op jit(solution)/shard_map/ppermute | solution.py:263
  27.1 2.1 %all-gather.1 = bf16[1536,128]{1,0:T(8,128)(2,1)S(1)} all-gather(bf16[768,128]{1,0:T(8,128)(2,1)S(1)} %pad_maximum_fusion.1), channel_id=3, replica_groups={{0,8},{16,24},{32,40},{48,56},{64,72},{80,88},{96,104},{112,120},{128,1..., dimensions={0}, use_global_device_ids=true | all-gather | bytes 589824 | tf_op jit(solution)/shard_map/all_gather | solution.py:266
  29.2 1.3 %own.1 = (bf16[896,128]{1,0:T(8,128)(2,1)S(1)}, bf16[896,128]{1,0:T(8,128)(2,1)S(1)}, f32[512,128]{1,0:T(8,128)S(1)}) custom-call(s32[1]{0:T(128)} %bitcast.core_ref, bf16[1056,128]{1,0:T(8,128)(2,1)S(1)} %slice_select_fusion.own_ref, bf16[512,256]{1,0:T(8,128)(2,1)S(1)} %collective-permute-done.1.behind_ref, ...), custom_call_target="tpu_custom_call" | custom-call | flops 201326592 | bytes 2000000 | tf_op jit(solution)/shard_map/own/pallas_call | solution.py:239
  30.5 0.0 collective-permute-done.ahead_ref
  30.5 0.8 %ahead.1 = bf16[512,128]{1,0:T(8,128)(2,1)S(1)} custom-call(bf16[1056,128]{1,0:T(8,128)(2,1)S(1)} %collective-permute-done.ahead_ref, bf16[896,128]{1,0:T(8,128)(2,1)S(1)} %get-tuple-element.8.keys7, bf16[896,128]{1,0:T(8,128)(2,1)S(1)} %get-tuple-element.9.values7, f32[512,128]{1,0:T(8,128)S(1)} %get-tuple-element.12.back_in), custom_call_target="tpu_custom_call" | custom-call | flops 100663296 | bytes 1000000 | tf_op jit(solution)/shard_map/ahead/pallas_call | solution.py:239
  31.3 3.7 %collective-permute-start.3 = (bf16[512,128]{1,0:T(8,128)(2,1)S(1)}, bf16[512,128]{1,0:T(8,128)(2,1)S(1)}, u32[]{:S(2)}, u32[]{:S(2)}) collective-permute-start(bf16[512,128]{1,0:T(8,128)(2,1)S(1)} %ahead.1), channel_id=1, source_target_pairs={{0,480},{8,488},{16,496},{24,504},{32,0},{40,8},{48,16},{56,24},{6... | collective-permute-start | bytes 393224 | tf_op jit(solution)/shard_map/ppermute | solution.py:263
  35.0 3.2 %after.1 = (bf16[256,128]{1,0:T(8,128)(2,1)S(1)}, f32[512,128]{1,0:T(8,128)S(1)}) custom-call(bf16[1056,128]{1,0:T(8,128)(2,1)S(1)} %slice_select_fusion.own_ref, bf16[1056,128]{1,0:T(8,128)(2,1)S(1)} %collective-permute-done.ahead_ref, bf16[896,128]{1,0:T(8,128)(2,1)S(1)} %get-tuple-element.8.keys7, bf16[896,128]{1,0:T(8,128)(2,1)S(1)} %get-tuple-element.9.values7), custom_call_target="tpu_custom_call" | custom-call | flops 402653184 | bytes 4000000 | tf_op jit(solution)/shard_map/after/pallas_call | solution.py:239
  38.2 0.1 collective-permute-done.3.back_ref
  38.3 2.4 %all-gather.2 = bf16[768,128]{1,0:T(8,128)(2,1)S(1)} all-gather(bf16[384,128]{1,0:T(8,128)(2,1)S(1)} %swap.1), channel_id=4, replica_groups={{0,8},{16,24},{32,40},{48,56},{64,72},{80,88},{96,104},{112,120},{128,1..., dimensions={0}, use_global_device_ids=true | all-gather | bytes 294912 | tf_op jit(solution)/shard_map/all_gather | solution.py:266
  40.8 0.7 %last.1 = (bf16[128,256]{1,0:T(8,128)(2,1)}, bf16[128,256]{1,0:T(8,128)(2,1)}, bf16[128,256]{1,0:T(8,128)(2,1)}) custom-call(s32[1]{0:T(128)} %bitcast.core_ref, bf16[256,128]{1,0:T(8,128)(2,1)S(1)} %get-tuple-element.10.query_grad, f32[512,128]{1,0:T(8,128)S(1)} %get-tuple-element.11.sums_ref, bf16[512,128]{1,0:T(8,128)(2,1)S(1)} %collective-permute-done.3.back_ref, ...), custom_call_target="tpu_custom_call" | custom-call | tf_op jit(solution)/shard_map/last/pallas_call | solution.py:239
  (7 shorter events, 0.1 us)
Async XLA Ops:
  2.3 20.6 %collective-permute-start.2 = (bf16[256,256]{1,0:T(8,128)(2,1)S(1)}, bf16[256,256]{1,0:T(8,128)(2,1)S(1)}, u32[]{:S(2)}, u32[]{:S(2)}) collective-permute-start(bf16[256,256]{1,0:T(8,128)(2,1)S(1)} %slice.27), channel_id=1, source_target_pairs={{8,56},{24,72},{40,88},{56,104},{72,120},{88,136},{104,152},{120,1... | collective-permute-start | bytes 393224 | tf_op jit(solution)/shard_map/ppermute | solution.py:263
  11.7 15.4 %collective-permute-start.1 = (bf16[512,256]{1,0:T(8,128)(2,1)S(1)}, bf16[512,256]{1,0:T(8,128)(2,1)S(1)}, u32[]{:S(2)}, u32[]{:S(2)}) collective-permute-start(bf16[512,256]{1,0:T(8,128)(2,1)S(1)} %bitcast.8), channel_id=1, source_target_pairs={{0,32},{8,24},{16,48},{24,40},{32,64},{40,56},{48,80},{56,72},{64,... | collective-permute-start | bytes 786440 | tf_op jit(solution)/shard_map/ppermute | solution.py:263
  14.9 15.7 %collective-permute-start = (bf16[1056,128]{1,0:T(8,128)(2,1)S(1)}, bf16[1056,128]{1,0:T(8,128)(2,1)S(1)}, u32[]{:S(2)}, u32[]{:S(2)}) collective-permute-start(bf16[1056,128]{1,0:T(8,128)(2,1)S(1)} %slice_select_fusion.own_ref), channel_id=1, source_target_pairs={{0,496},{8,504},{16,0},{24,8},{32,16},{40,24},{48,32},{56,40},{64,... | collective-permute-start | bytes 811016 | tf_op jit(solution)/shard_map/ppermute | solution.py:263
  31.3 7.0 %collective-permute-start.3 = (bf16[512,128]{1,0:T(8,128)(2,1)S(1)}, bf16[512,128]{1,0:T(8,128)(2,1)S(1)}, u32[]{:S(2)}, u32[]{:S(2)}) collective-permute-start(bf16[512,128]{1,0:T(8,128)(2,1)S(1)} %ahead.1), channel_id=1, source_target_pairs={{0,480},{8,488},{16,496},{24,504},{32,0},{40,8},{48,16},{56,24},{6... | collective-permute-start | bytes 393224 | tf_op jit(solution)/shard_map/ppermute | solution.py:263

commit v6 on v5

--- a/solution.py
+++ b/solution.py
@@ -169,12 +169,14 @@
     return step
 
 
-def ahead_kernel(ahead_ref, keys7, values7, back_in, back_out, keys, values):
-    for target, source, part in ((keys, keys7, 0), (values, values7, 1)):
-        target[: 5 * ROWS, :] = source[2 * ROWS :, :]
-        target[5 * ROWS :, :] = block_of(ahead_ref, 0)[part]
+def ahead_kernel(ahead_ref, keys7, values7, back_in, back_out):
+    block = block_of(ahead_ref, 0)
+    strips = [
+        jnp.concatenate([ref[2 * ROWS :, :], block[part]], axis=0)
+        for part, ref in enumerate((keys7, values7))
+    ]
     sums = read_sums(back_in, 1)
-    strip_step(2, 2, block_of(ahead_ref, 0), keys, values, [0], sums)
+    dots(query_step(*strips, *block[2:], [0]), 0, sums, 2)
     write_sums(back_out, sums, 1)
 
 
@@ -285,7 +287,7 @@
     )
     (back,) = call(
         ahead_kernel, "ahead", [(sums_of, bf16)], (ahead, keys7, values7, back),
-        (6 * ROWS, 6 * ROWS), work=1, scalar=False,
+        work=1, scalar=False,
     )
     returned = send(back, -2, -2)
     query_grad, sums = call(

time: 41.7 us -> 41.7 us (level)
  no operation moved by 1% of the time
where the time goes in v6:
time: 41.7 us; the launch traced here: 41.5 us
  starting transfers between devices  21.6 us (52%)
  blocking collectives  7.07 us (17%)
  Pallas kernels  6.04 us (14%)
  waiting for transfers between devices  4.3 us (10%)
  other arithmetic  1.68 us (4%)
  between operations  0.75 us (2%)
    ppermute x4, starting transfers between devices, send(): return lax.ppermute(value, 'tm', pairs)  21.6 us
    all_gather x3, blocking collectives, share(): return lax.all_gather(value, 'tm', axis_index_groups=cores)  7.07 us
    pallas_call x6, Pallas kernels, call(): pl.pallas_call(kernel, name=name, out_shape=outs, in_specs=[SMEM] * scala...  6.04 us
    ppermute x4, waiting for transfers between devices, send(): return lax.ppermute(value, 'tm', pairs)  4.3 us
    max x1, other arithmetic, placed(): total = padded if total is None else jnp.maximum(total, padded)  0.95 us
  transfers between devices with their start and end apart: 4, of which 2 were waited for; matrix products, arithmetic and copies ran while one was open for 0% of the time, Pallas kernels for 11%

profile of v6, /device:TPU:1, one launch (start us, length us, event | category | flops | bytes accessed | tf_op | source)
XLA Modules:
  0.0 41.5 jit_solution(8796208863172088750)
XLA Ops:
  0.6 0.7 %compare_convert_fusion = bf16[1,6]{1,0:T(2,128)(2,1)S(1)} fusion(s32[1,6]{1,0:T(1,128)} %param.9), kind=kLoop, calls=%fused_computation.4 | loop fusion | flops 12 | bytes 36 | tf_op jit(solution)/shard_map/convert_element_type | solution.py:273
  1.3 1.0 %pad_maximum_fusion = bf16[528,256]{1,0:T(8,128)(2,1)S(1)} fusion(bf16[1,6]{1,0:T(2,128)(2,1)S(1)} %compare_convert_fusion, bf16[128,256]{1,0:T(8,128)(2,1)} %param.8, bf16[128,256]{1,0:T(8,128)(2,1)} %param.5, bf16[128,256]{1,0:T(8,128)(2,1)} %param.7, bf16[128,256]{1,0:T(8,128)(2,1)} %param.6), kind=kLoop, calls=%fused_computation.1 | loop fusion | flops 1622016 | bytes 532492 | tf_op jit(solution)/shard_map/max | solution.py:28
  2.3 6.8 %collective-permute-start.2 = (bf16[256,256]{1,0:T(8,128)(2,1)S(1)}, bf16[256,256]{1,0:T(8,128)(2,1)S(1)}, u32[]{:S(2)}, u32[]{:S(2)}) collective-permute-start(bf16[256,256]{1,0:T(8,128)(2,1)S(1)} %slice.27), channel_id=1, source_target_pairs={{8,56},{24,72},{40,88},{56,104},{72,120},{88,136},{104,152},{120,1... | collective-permute-start | bytes 393224 | tf_op jit(solution)/shard_map/ppermute | solution.py:265
  9.1 2.5 %all-gather = bf16[1056,256]{1,0:T(8,128)(2,1)S(1)} all-gather(bf16[528,256]{1,0:T(8,128)(2,1)S(1)} %pad_maximum_fusion), channel_id=2, replica_groups={{0,8},{16,24},{32,40},{48,56},{64,72},{80,88},{96,104},{112,120},{128,1..., dimensions={0}, use_global_device_ids=true | all-gather | bytes 811008 | tf_op jit(solution)/shard_map/all_gather | solution.py:268
  11.7 3.2 %collective-permute-start.1 = (bf16[512,256]{1,0:T(8,128)(2,1)S(1)}, bf16[512,256]{1,0:T(8,128)(2,1)S(1)}, u32[]{:S(2)}, u32[]{:S(2)}) collective-permute-start(bf16[512,256]{1,0:T(8,128)(2,1)S(1)} %bitcast.8), channel_id=1, source_target_pairs={{0,32},{8,24},{16,48},{24,40},{32,64},{40,56},{48,80},{56,72},{64,... | collective-permute-start | bytes 786440 | tf_op jit(solution)/shard_map/ppermute | solution.py:265
  14.9 7.9 %collective-permute-start = (bf16[1056,128]{1,0:T(8,128)(2,1)S(1)}, bf16[1056,128]{1,0:T(8,128)(2,1)S(1)}, u32[]{:S(2)}, u32[]{:S(2)}) collective-permute-start(bf16[1056,128]{1,0:T(8,128)(2,1)S(1)} %slice_select_fusion.own_ref), channel_id=1, source_target_pairs={{0,496},{8,504},{16,0},{24,8},{32,16},{40,24},{48,32},{56,40},{64,... | collective-permute-start | bytes 811016 | tf_op jit(solution)/shard_map/ppermute | solution.py:265
  22.8 0.0 collective-permute-done.2.value_ref.far_ref
  22.9 4.2 %collective-permute-done.1.behind_ref = bf16[512,256]{1,0:T(8,128)(2,1)S(1)} collective-permute-done((bf16[512,256]{1,0:T(8,128)(2,1)S(1)}, bf16[512,256]{1,0:T(8,128)(2,1)S(1)}, u32[]{:S(2)}, u32[]{:S(2)}) %collective-permute-start.1) | collective-permute-done | bytes 262176 | tf_op jit(solution)/shard_map/ppermute | solution.py:265
  27.1 2.1 %all-gather.1 = bf16[1536,128]{1,0:T(8,128)(2,1)S(1)} all-gather(bf16[768,128]{1,0:T(8,128)(2,1)S(1)} %pad_maximum_fusion.1), channel_id=3, replica_groups={{0,8},{16,24},{32,40},{48,56},{64,72},{80,88},{96,104},{112,120},{128,1..., dimensions={0}, use_global_device_ids=true | all-gather | bytes 589824 | tf_op jit(solution)/shard_map/all_gather | solution.py:268
  29.2 1.3 %own.1 = (bf16[896,128]{1,0:T(8,128)(2,1)S(1)}, bf16[896,128]{1,0:T(8,128)(2,1)S(1)}, f32[512,128]{1,0:T(8,128)S(1)}) custom-call(s32[1]{0:T(128)} %bitcast.core_ref, bf16[1056,128]{1,0:T(8,128)(2,1)S(1)} %slice_select_fusion.own_ref, bf16[512,256]{1,0:T(8,128)(2,1)S(1)} %collective-permute-done.1.behind_ref, ...), custom_call_target="tpu_custom_call" | custom-call | flops 201326592 | bytes 2000000 | tf_op jit(solution)/shard_map/own/pallas_call | solution.py:241
  30.5 0.0 collective-permute-done.ahead_ref
  30.5 0.8 %ahead.1 = bf16[512,128]{1,0:T(8,128)(2,1)S(1)} custom-call(bf16[1056,128]{1,0:T(8,128)(2,1)S(1)} %collective-permute-done.ahead_ref, bf16[896,128]{1,0:T(8,128)(2,1)S(1)} %get-tuple-element.8.keys7, bf16[896,128]{1,0:T(8,128)(2,1)S(1)} %get-tuple-element.9.values7, f32[512,128]{1,0:T(8,128)S(1)} %get-tuple-element.12.back_in), custom_call_target="tpu_custom_call" | custom-call | flops 100663296 | bytes 1000000 | tf_op jit(solution)/shard_map/ahead/pallas_call | solution.py:241
  31.3 3.7 %collective-permute-start.3 = (bf16[512,128]{1,0:T(8,128)(2,1)S(1)}, bf16[512,128]{1,0:T(8,128)(2,1)S(1)}, u32[]{:S(2)}, u32[]{:S(2)}) collective-permute-start(bf16[512,128]{1,0:T(8,128)(2,1)S(1)} %ahead.1), channel_id=1, source_target_pairs={{0,480},{8,488},{16,496},{24,504},{32,0},{40,8},{48,16},{56,24},{6... | collective-permute-start | bytes 393224 | tf_op jit(solution)/shard_map/ppermute | solution.py:265
  35.0 3.2 %after.1 = (bf16[256,128]{1,0:T(8,128)(2,1)S(1)}, f32[512,128]{1,0:T(8,128)S(1)}) custom-call(bf16[1056,128]{1,0:T(8,128)(2,1)S(1)} %slice_select_fusion.own_ref, bf16[1056,128]{1,0:T(8,128)(2,1)S(1)} %collective-permute-done.ahead_ref, bf16[896,128]{1,0:T(8,128)(2,1)S(1)} %get-tuple-element.8.keys7, bf16[896,128]{1,0:T(8,128)(2,1)S(1)} %get-tuple-element.9.values7), custom_call_target="tpu_custom_call" | custom-call | flops 402653184 | bytes 4000000 | tf_op jit(solution)/shard_map/after/pallas_call | solution.py:241
  38.2 0.1 collective-permute-done.3.back_ref
  38.3 2.4 %all-gather.2 = bf16[768,128]{1,0:T(8,128)(2,1)S(1)} all-gather(bf16[384,128]{1,0:T(8,128)(2,1)S(1)} %swap.1), channel_id=4, replica_groups={{0,8},{16,24},{32,40},{48,56},{64,72},{80,88},{96,104},{112,120},{128,1..., dimensions={0}, use_global_device_ids=true | all-gather | bytes 294912 | tf_op jit(solution)/shard_map/all_gather | solution.py:268
  40.8 0.7 %last.1 = (bf16[128,256]{1,0:T(8,128)(2,1)}, bf16[128,256]{1,0:T(8,128)(2,1)}, bf16[128,256]{1,0:T(8,128)(2,1)}) custom-call(s32[1]{0:T(128)} %bitcast.core_ref, bf16[256,128]{1,0:T(8,128)(2,1)S(1)} %get-tuple-element.10.query_grad, f32[512,128]{1,0:T(8,128)S(1)} %get-tuple-element.11.sums_ref, bf16[512,128]{1,0:T(8,128)(2,1)S(1)} %collective-permute-done.3.back_ref, ...), custom_call_target="tpu_custom_call" | custom-call | tf_op jit(solution)/shard_map/last/pallas_call | solution.py:241
  (7 shorter events, 0.1 us)
Async XLA Ops:
  2.3 20.6 %collective-permute-start.2 = (bf16[256,256]{1,0:T(8,128)(2,1)S(1)}, bf16[256,256]{1,0:T(8,128)(2,1)S(1)}, u32[]{:S(2)}, u32[]{:S(2)}) collective-permute-start(bf16[256,256]{1,0:T(8,128)(2,1)S(1)} %slice.27), channel_id=1, source_target_pairs={{8,56},{24,72},{40,88},{56,104},{72,120},{88,136},{104,152},{120,1... | collective-permute-start | bytes 393224 | tf_op jit(solution)/shard_map/ppermute | solution.py:265
  11.7 15.4 %collective-permute-start.1 = (bf16[512,256]{1,0:T(8,128)(2,1)S(1)}, bf16[512,256]{1,0:T(8,128)(2,1)S(1)}, u32[]{:S(2)}, u32[]{:S(2)}) collective-permute-start(bf16[512,256]{1,0:T(8,128)(2,1)S(1)} %bitcast.8), channel_id=1, source_target_pairs={{0,32},{8,24},{16,48},{24,40},{32,64},{40,56},{48,80},{56,72},{64,... | collective-permute-start | bytes 786440 | tf_op jit(solution)/shard_map/ppermute | solution.py:265
  14.9 15.7 %collective-permute-start = (bf16[1056,128]{1,0:T(8,128)(2,1)S(1)}, bf16[1056,128]{1,0:T(8,128)(2,1)S(1)}, u32[]{:S(2)}, u32[]{:S(2)}) collective-permute-start(bf16[1056,128]{1,0:T(8,128)(2,1)S(1)} %slice_select_fusion.own_ref), channel_id=1, source_target_pairs={{0,496},{8,504},{16,0},{24,8},{32,16},{40,24},{48,32},{56,40},{64,... | collective-permute-start | bytes 811016 | tf_op jit(solution)/shard_map/ppermute | solution.py:265
  31.3 7.0 %collective-permute-start.3 = (bf16[512,128]{1,0:T(8,128)(2,1)S(1)}, bf16[512,128]{1,0:T(8,128)(2,1)S(1)}, u32[]{:S(2)}, u32[]{:S(2)}) collective-permute-start(bf16[512,128]{1,0:T(8,128)(2,1)S(1)} %ahead.1), channel_id=1, source_target_pairs={{0,480},{8,488},{16,496},{24,504},{32,0},{40,8},{48,16},{56,24},{6... | collective-permute-start | bytes 393224 | tf_op jit(solution)/shard_map/ppermute | solution.py:265
